TPU v7x, 512 devices: a whole 4x4x16 slice. The times are simulated.
512 devices in a mesh: inst: 32 (over y_hi, z), tp: 16 (over x, y_lo, core).
Axes of the slice: x: 4, y: 4 (y_hi: 2, y_lo: 2; y = y_hi * 2 + y_lo), z: 16, core: 2. Of those that a mesh axis runs over, the one named last changes fastest.
Arguments:
- queries: bfloat16 [2, 3072, 64, 128], P(None, 'inst', 'tp'), may hold values from -8 to 50
- row_prompt: int32 [3072], P('inst'), may hold values from 0 to 47, as said below
- owner_slot: int32 [48], replicated, may hold values from 0 to 63, as said below
- suffix_len: int32 [3072], P('inst'), may hold values from 1 to 8
- prefix_keys: bfloat16 [64, 4096, 16, 128], P('inst', None, 'tp'), may hold values from -4.5 to 50, as said below
- prefix_values: bfloat16 [64, 4096, 16, 128], P('inst', None, 'tp'), may hold values from -8 to 8, as said below
- suffix_keys: bfloat16 [3072, 8, 16, 128], P('inst', None, 'tp'), may hold values from -12 to 12, as said below
- suffix_values: bfloat16 [3072, 8, 16, 128], P('inst', None, 'tp'), may hold values from -8 to 8, as said below
- new_keys: bfloat16 [2, 3072, 16, 128], P(None, 'inst', 'tp'), may hold values from -12 to 12, as said below
- new_values: bfloat16 [2, 3072, 16, 128], P(None, 'inst', 'tp'), may hold values from -8 to 8, as said below
- out_weight: bfloat16 [8192, 2560], P('tp'), may hold values from -0.0625 to 0.0625
Outputs:
- projected: bfloat16 [3072, 2, 2560], P(('inst', 'tp'))
Inputs may be any that keep to these rules, and one draw needn't show every extreme that they name: `row_prompt`: samples come in consecutive blocks of 64, one prompt each, every prompt in exactly one block. `owner_slot`: different prompts have different slots. `prefix_keys`: copies of one key-value head are equal. `prefix_values`: copies of one key-value head are equal. `suffix_keys`: copies of one key-value head are equal. `suffix_values`: copies of one key-value head are equal. `new_keys`: copies of one key-value head are equal. `new_values`: copies of one key-value head are equal.
All inputs are finite; a program needn't handle non-finite values.
Results may differ from a plain program's by a relative error of at most 0.0052.
Values may be sent and summed in bfloat16 or wider, within the bound.
A program may use at most 128 MiB of HBM per device.

v0:
```python
import math

import jax
import jax.numpy as jnp
from jax import lax
from jax.sharding import PartitionSpec as P

GROUP = 64


def prefix_part(query_block, key_block, value_block):
    step_count, row_count, head_count, head_width = query_block.shape
    copy_count = key_block.shape[1]
    grouped = query_block.reshape(
        step_count, row_count, copy_count, head_count // copy_count, head_width
    )
    scores = jnp.einsum(
        "tbcrd,pcd->tbcrp", grouped, key_block, preferred_element_type=jnp.float32
    ) / math.sqrt(head_width)
    highest = jnp.max(scores, axis=-1)
    weights_raw = jnp.exp(scores - highest[..., None])
    weight_sum = jnp.sum(weights_raw, axis=-1)
    summed = jnp.einsum(
        "tbcrp,pcd->tbcrd",
        weights_raw.astype(jnp.bfloat16),
        value_block,
        preferred_element_type=jnp.float32,
    )
    output = (
        (summed / weight_sum[..., None])
        .astype(jnp.bfloat16)
        .reshape(step_count, row_count, head_count, head_width)
    )
    log_total = (highest + jnp.log(weight_sum)).reshape(step_count, row_count, head_count)
    return (output, log_total)


def combine(
    queries, prefix_out, prefix_total, suffix_len, suffix_keys, suffix_values, new_keys, new_values
):
    step_count, row_count, head_count, head_width = queries.shape
    copy_count = suffix_keys.shape[2]
    cache_len = suffix_keys.shape[1]
    all_keys = jnp.concatenate([suffix_keys, jnp.swapaxes(new_keys, 0, 1)], axis=1)
    all_values = jnp.concatenate([suffix_values, jnp.swapaxes(new_values, 0, 1)], axis=1)
    grouped = queries.reshape(
        step_count, row_count, copy_count, head_count // copy_count, head_width
    )
    scores = jnp.einsum(
        "trcxd,rjcd->trcxj", grouped, all_keys, preferred_element_type=jnp.float32
    ) / math.sqrt(head_width)
    key_slots = jnp.arange(cache_len + step_count)
    step_ids = jnp.arange(step_count)
    live = jnp.where(
        key_slots[None, None, :] < cache_len,
        key_slots[None, None, :] < suffix_len[None, :, None],
        key_slots[None, None, :] - cache_len <= step_ids[:, None, None],
    )
    masked = jnp.where(live[:, :, None, None, :], scores, -jnp.inf)
    carried = prefix_total.reshape(step_count, row_count, copy_count, head_count // copy_count)
    highest = jnp.maximum(carried, jnp.max(masked, axis=-1))
    weights_raw = jnp.exp(masked - highest[..., None])
    share = jnp.exp(carried - highest)
    denominator = share + jnp.sum(weights_raw, axis=-1)
    mixed = jnp.einsum(
        "trcxj,rjcd->trcxd",
        weights_raw.astype(jnp.bfloat16),
        all_values,
        preferred_element_type=jnp.float32,
    )
    earlier = prefix_out.reshape(
        step_count, row_count, copy_count, head_count // copy_count, head_width
    ).astype(jnp.float32)
    numerator = share[..., None] * earlier + mixed
    attended = (numerator / denominator[..., None]).astype(jnp.bfloat16)
    return attended.reshape(step_count, row_count, head_count * head_width)


def shards(
    queries,
    row_prompt,
    owner_slot,
    suffix_len,
    prefix_keys,
    prefix_values,
    suffix_keys,
    suffix_values,
    new_keys,
    new_values,
    out_weight,
):
    step_count, local_rows, head_count, head_width = queries.shape
    owned_count = prefix_keys.shape[0]
    inst_index = lax.axis_index("inst")
    row_start = inst_index * local_rows
    global_rows = row_start + jnp.arange(local_rows, dtype=jnp.int32)
    query_all, prompt_all = (
        lax.all_gather(queries, "inst", axis=1, tiled=True),
        lax.all_gather(row_prompt, "inst", axis=0, tiled=True),
    )
    slot_ids = inst_index * owned_count + jnp.arange(owned_count, dtype=jnp.int32)
    matches = owner_slot[None, :] == slot_ids[:, None]
    owned_prompt = jnp.argmax(matches, axis=1)
    first_rows = jnp.argmax(prompt_all[None, :] == owned_prompt[:, None], axis=1)
    outputs = []
    totals = []
    for owned_index in range(owned_count):
        query_block = lax.dynamic_slice_in_dim(query_all, first_rows[owned_index], GROUP, 1)
        part_out, part_total = prefix_part(
            query_block, prefix_keys[owned_index], prefix_values[owned_index]
        )
        outputs.append(part_out)
        totals.append(part_total)
    result_all = lax.all_gather(jnp.stack(outputs), "inst", axis=0, tiled=True)
    total_all = lax.all_gather(jnp.stack(totals), "inst", axis=0, tiled=True)
    row_slot = owner_slot[row_prompt]
    offsets = global_rows % GROUP
    prefix_out = jnp.moveaxis(result_all[row_slot, :, offsets], 0, 1)
    prefix_total = jnp.moveaxis(total_all[row_slot, :, offsets], 0, 1)
    attended = combine(
        queries,
        prefix_out,
        prefix_total,
        suffix_len,
        suffix_keys,
        suffix_values,
        new_keys,
        new_values,
    )
    by_row = jnp.swapaxes(attended, 0, 1)
    summed = lax.psum_scatter(
        jnp.einsum("rtk,kd->rtd", by_row, out_weight, preferred_element_type=jnp.float32),
        "tp",
        scatter_dimension=0,
        tiled=True,
    )
    return summed.astype(jnp.bfloat16)


def solution(mesh):
    placed = (
        P(None, "inst", "tp", None),
        P("inst"),
        P(),
        P("inst"),
        P("inst", None, "tp", None),
        P("inst", None, "tp", None),
        P("inst", None, "tp", None),
        P("inst", None, "tp", None),
        P(None, "inst", "tp", None),
        P(None, "inst", "tp", None),
        P("tp", None),
    )
    return jax.shard_map(
        shards, mesh=mesh, in_specs=placed, out_specs=P(("inst", "tp"), None, None), check_vma=False
    )
```

profile of v0, /device:TPU:1, one launch (start us, length us, event | category | flops | bytes accessed | tf_op | source)
XLA Modules:
  0.0 490.7 jit_solution(5471473537550955053)
XLA Ops:
  6.5 1.8 copy.44
  8.4 1.3 dynamic-slice
  10.3 0.9 dynamic-update-slice
  11.2 128.0 %all-reduce = s32[3072]{0:T(1024)S(1)} all-reduce(s32[3072]{0:T(1024)S(1)} %dynamic-update-slice), channel_id=1, replica_groups=mesh['inst'=32,'tp'=16] {'inst'}, use_global_device_ids=true, to_apply=%add | all-reduce | flops 3072 | bytes 24576
  139.2 1.4 compare_reduce_fusion.1
  140.6 0.7 compare_reduce_fusion
  141.3 0.6 fusion.83
  145.8 40.9 %all-gather.3.cloned.1.call-done = bf16[2,3072,4,128]{3,1,2,0:T(8,128)(2,1)} async-done(((bf16[2,96,4,128]{3,1,2,0:T(8,128)(2,1)}), bf16[2,3072,4,128]{3,1,2,0:T(8,128)(2,1)}) %all-gather.3.cloned.1.call-update) | async-done | bytes 6291472 | tf_op jit(solution)/shard_map/all_gather | solution.py:98
  186.7 2.8 bitcast_reduce_fusion
  189.5 1.5 fusion.5
  191.0 1.5 fusion.40
  192.4 2.3 bitcast_reduce_fusion.1
  194.8 1.5 fusion.3
  196.3 1.5 fusion.31
  197.8 0.7 pad_maximum_fusion
  198.6 1.2 gather_fusion
  199.9 1.3 dynamic-slice.1
  202.1 1.4 fusion.84
  203.6 60.5 %all_gather.14 = f32[64,2,64,4]{2,3,1,0:T(4,128)S(1)} all-gather(f32[2,2,64,4]{2,3,1,0:T(4,128)S(1)} %pad_maximum_fusion.1), channel_id=1, replica_groups=mesh['inst'=32,'tp'=16] {'inst'}, dimensions={0}, use_global_device_ids=true | all-gather | bytes 135168 | tf_op jit(solution)/shard_map/all_gather | solution.py:115
  264.1 3.9 copy.45
  268.0 3.4 gather_fusion.1
  271.5 0.6 fusion.57
  272.1 0.8 fusion.81
  272.9 114.6 %all-gather.5.cloned.1.call-done = bf16[64,2,64,4,128]{4,2,3,1,0:T(8,128)(2,1)} async-done(((bf16[2,2,64,4,128]{4,2,3,1,0:T(8,128)(2,1)}), bf16[64,2,64,4,128]{4,2,3,1,0:T(8,128)(2,1)}) %all-gather.5.cloned.1.call-update) | async-done | bytes 8388624 | tf_op jit(solution)/shard_map/all_gather | solution.py:114
  387.4 11.0 %copy.49 = bf16[64,2,64,4,128]{4,3,2,1,0:T(4,128)(2,1)} copy(bf16[64,2,64,4,128]{4,2,3,1,0:T(8,128)(2,1)} %all-gather.5.cloned.1.call-done) | data formatting | bytes 16777216 | tf_op jit(solution)/shard_map/all_gather | solution.py:114
  398.5 4.6 gather_fusion.2
  403.1 2.4 fusion.17
  405.5 1.0 reshape.314
  406.5 0.7 fusion.12
  407.2 2.8 copy.53
  410.0 72.3 %all-reduce.3 = bf16[96,2,2560]{2,1,0:T(2,128)(2,1)} all-reduce(f32[96,2,2560]{2,1,0:T(2,128)} %copy.53), channel_id=2, replica_groups=mesh['inst'=32,'tp'=16] {'tp'}, use_global_device_ids=true, to_apply=%region_8.9.clone | all-reduce | flops 491520 | bytes 2949120
  482.3 1.5 dynamic-slice_convert_fusion
  (39 shorter events, 0.5 us)
Async XLA Ops:
  6.5 400.0 %copy-start = (bf16[512,2560]{1,0:T(8,128)(2,1)S(1)}, bf16[512,2560]{1,0:T(8,128)(2,1)}, u32[]{:S(2)}) copy-start(bf16[512,2560]{1,0:T(8,128)(2,1)} %param.21) | copy-start | bytes 7864324
  6.5 180.1 %all-gather.3.cloned.1.call-start = ((), (), s32[]{:S(2)}) async-start(), calls=%async_computation | async-start | bytes 6488064 | tf_op jit(solution)/shard_map/all_gather | solution.py:98
  8.3 379.1 %all-gather.5.cloned.1.call-start = ((), (), s32[]{:S(2)}) async-start(), calls=%async_computation.1 | async-start | bytes 8650752 | tf_op jit(solution)/shard_map/all_gather | solution.py:114
  186.7 4.3 copy-start.8
  189.4 3.0 copy-start.2
  194.7 3.8 copy-start.5
  194.7 3.9 copy-start.9
  194.7 3.9 copy-start.1
  194.8 5.1 %copy-start.6 = (bf16[2,96,1,128]{3,1,2,0:T(8,128)(2,1)S(1)}, bf16[2,96,1,128]{3,1,2,0:T(8,128)(2,1)}, u32[]{:S(2)}) copy-start(bf16[2,96,1,128]{3,1,2,0:T(8,128)(2,1)} %param.19) | copy-start | bytes 147460
  194.8 7.2 %copy-start.7 = (s32[96]{0:T(128)S(1)}, s32[96]{0:T(128)}, u32[]{:S(2)}) copy-start(s32[96]{0:T(128)} %param.14) | copy-start | bytes 1156
  194.8 7.3 %copy-start.3 = (bf16[2,96,4,128]{3,2,1,0:T(4,128)(2,1)S(1)}, bf16[2,96,4,128]{3,2,1,0:T(4,128)(2,1)}, u32[]{:S(2)}) copy-start(bf16[2,96,4,128]{3,2,1,0:T(4,128)(2,1)} %param.11) | copy-start | bytes 589828
  272.9 130.3 %copy-start.4 = (f32[2,96,4]{2,0,1:T(2,128)S(1)}, f32[2,96,4]{2,0,1:T(2,128)}, u32[]{:S(2)}) copy-start(f32[2,96,4]{2,0,1:T(2,128)} %get-tuple-element.9) | copy-start | bytes 9220
Sparse Core Ops, SparseCore 0:
  10.5 176.1 all-gather.2
  198.6 188.7 all-gather.4
where the time goes:
time: 493 us; the launch traced here: 491 us
  blocking collectives  261 us (53%)
  waiting for transfers between devices  156 us (32%)
  local copies, waits for them, and re-layouts  35.5 us (7%)
  between operations  18.9 us (4%)
  matrix products  12.5 us (3%)
  other arithmetic  7.46 us (2%)
    unnamed x2, blocking collectives  200 us
    all_gather x1, waiting for transfers between devices, shards(): result_all = lax.all_gather(jnp.stack(outputs), 'inst', axis=0, tiled=True)  115 us
    all_gather x1, blocking collectives, shards(): total_all = lax.all_gather(jnp.stack(totals), 'inst', axis=0, tiled=True)  60.5 us
    all_gather x1, waiting for transfers between devices, shards(): lax.all_gather(queries, 'inst', axis=1, tiled=True)  40.9 us
    all_gather x1, local copies, waits for them, and re-layouts, shards(): result_all = lax.all_gather(jnp.stack(outputs), 'inst', axis=0, tiled=True)  11 us
  transfers between devices with their start and end apart: 2, of which 2 were waited for; matrix products, arithmetic and copies ran while one was open for 4% of the time, Pallas kernels for 0%

commit v1 on v0

v1 whole, which is shorter than its diff:
```python
import math

import jax
import jax.numpy as jnp
from jax import lax
from jax.experimental import pallas as pl
from jax.experimental.pallas import tpu as pltpu
from jax.sharding import PartitionSpec as P

F32 = jnp.float32
BF16 = jnp.bfloat16
I32 = jnp.int32

NI = 32
NZ = 16
HALVES = 3
BLOCKS = 48
SLOTS = 64
OWN = 2
HD = 128
KEYS = 4096
D = 2560
CH = 512
NCH = D // CH
KC = 512
SCALE = 1.0 / math.sqrt(HD)
C2 = SCALE * math.log2(math.e)
NEG = -1e30


def dot_t(a, b):
    return lax.dot_general(a, b, (((1,), (1,)), ((), ())), preferred_element_type=F32)


def dot(a, b):
    return lax.dot_general(a, b, (((1,), (0,)), ((), ())), preferred_element_type=F32)


def iota(shape, dim):
    return lax.broadcasted_iota(I32, shape, dim)


def kernel(
    row_prompt,
    owner_slot,
    lens,
    q_hbm,
    k_hbm,
    v_hbm,
    sk_hbm,
    sv_hbm,
    nk_hbm,
    nv_hbm,
    w_hbm,
    out,
    q,
    kk,
    va,
    ck,
    cv,
    w,
    tab,
    inv_v,
    inv_s,
    mid,
    snd,
    qin,
    scores,
    obuf,
    tbuf,
    mid2,
    tmid,
    snd2,
    tsnd,
    pin,
    tin,
    own_acc,
    own_m,
    own_l,
    att,
    lhs,
    mine,
    cs,
    cr,
    xs,
    xr,
    sums,
    ld,
    ss,
    rs,
    css,
    crs,
    xss,
    xrs,
):
    inst = lax.axis_index("inst")
    tp = lax.axis_index("tp")
    yy = lax.div(inst, NZ)
    zz = lax.rem(inst, NZ)
    core = lax.rem(tp, 2)
    chip = lax.div(tp, 2)
    partner = tp + 1 - 2 * core

    def remote(src, dst, s, r, **where):
        return pltpu.make_async_remote_copy(
            src_ref=src, dst_ref=dst, send_sem=s, recv_sem=r,
            device_id=where, device_id_type=pl.DeviceIdType.MESH,
        )

    def local(src, dst, s):
        return pltpu.make_async_copy(src, dst, s)

    def chip_at(step):
        return lax.rem(chip + step, 8) * 2 + core

    load_q = local(q_hbm, q, ld.at[0])
    load_q.start()
    loads_own = []
    for u in range(HALVES):
        for src, dst, sem in ((sk_hbm, ck, 3), (sv_hbm, cv, 4)):
            loads_own.append(
                local(src.at[pl.ds(256 * u, 256)], dst.at[u, pl.ds(0, 256)], ld.at[sem + 4 * u])
            )
        for src, dst, sem in ((nk_hbm, ck, 5), (nv_hbm, cv, 6)):
            loads_own.append(
                local(
                    src.at[:, pl.ds(32 * u, 32)],
                    dst.at[u, pl.ds(256, 64)].reshape(2, 32, HD),
                    ld.at[sem + 4 * u],
                )
            )
    for c in loads_own:
        c.start()
    load_k = local(k_hbm, kk, ld.at[1])
    load_k.start()
    load_v = local(v_hbm, va.at[:, :, pl.ds(0, HD)], ld.at[2])
    load_v.start()
    load_w = local(w_hbm, w, ld.at[15])
    load_w.start()

    barrier = pltpu.get_barrier_semaphore()

    def greet(n, _):
        pl.semaphore_signal(
            barrier, inc=1, device_id={"inst": lax.rem(inst + n, NI)},
            device_id_type=pl.DeviceIdType.MESH,
        )
        return 0

    lax.fori_loop(1, NI, greet, 0)
    pl.semaphore_signal(
        barrier, inc=1, device_id={"tp": partner}, device_id_type=pl.DeviceIdType.MESH
    )

    def greet_chip(n, _):
        pl.semaphore_signal(
            barrier, inc=1, device_id={"tp": chip_at(n)}, device_id_type=pl.DeviceIdType.MESH
        )
        return 0

    lax.fori_loop(1, 8, greet_chip, 0)

    rows4 = iota((4, HD), 0)
    head = jnp.full((4, HD), 255, I32)
    for u in range(HALVES):
        head = jnp.where(rows4 == u, owner_slot[row_prompt[32 * u]], head)
    tab[inst] = head
    ones = jnp.ones((256, HD), BF16)

    def set_ones(n, _):
        va[lax.div(n, 16), pl.ds(pl.multiple_of(lax.rem(n, 16) * 256, 256), 256), pl.ds(HD, HD)] = ones
        return 0

    lax.fori_loop(0, 32, set_ones, 0)
    for u in range(HALVES):
        ck[u, pl.ds(320, 64)] = jnp.zeros((64, HD), BF16)
        cv[u, pl.ds(320, 64)] = jnp.zeros((64, HD), BF16)

    pl.semaphore_wait(barrier, NI - 1 + 1 + 7)

    def send_head(n, _):
        remote(
            tab.at[inst], tab.at[inst], ss.at[0], rs.at[0], inst=lax.rem(inst + n, NI)
        ).start()
        return 0

    lax.fori_loop(1, NI, send_head, 0)

    load_q.wait()

    def piece_of(u, m):
        t = lax.div(m, 8)
        at = pl.multiple_of(128 * u + 16 * lax.rem(m, 8), 16)
        return q.at[t, pl.ds(at, 16)]

    def block_at(u):
        return lax.div(HALVES * inst + u, 2)

    for u in range(HALVES):
        side = lax.rem(zz + u, 2)

        @pl.when(side == yy)
        def _():
            local(piece_of(u, zz), mid.at[block_at(u)], rs.at[1]).start()

        @pl.when(side != yy)
        def _():
            remote(piece_of(u, zz), mid.at[block_at(u)], ss.at[1], rs.at[1], inst=side * NZ + zz).start()

    def send_piece(n, _):
        m = lax.rem(zz + n, NZ)
        for u in range(HALVES):
            side = lax.rem(zz + u, 2)
            remote(piece_of(u, m), mid.at[block_at(u)], ss.at[1], rs.at[1], inst=side * NZ + m).start()
        return 0

    lax.fori_loop(1, NZ, send_piece, 0)

    for c in loads_own:
        c.wait()
    lens_b = jnp.broadcast_to(lens[...].astype(F32), (8, 96)).astype(BF16)
    for u in range(HALVES):
        at96 = iota((96, 384), 0)
        lane96 = iota((96, 384), 1)
        spread = jnp.where(at96 == 32 * u + lax.div(lane96, 8), 1.0, 0.0).astype(BF16)
        len_row = dot(lens_b, spread)[0:1]
        row = iota((256, 384), 0)
        lane = iota((256, 384), 1)
        sample = lax.div(lax.rem(row, 128), 4)
        step = lax.div(row, 128)
        cached = (lane < 256) & (lax.div(lane, 8) == sample) & (
            lax.rem(lane, 8).astype(F32) < jnp.broadcast_to(len_row, (256, 384))
        )
        new_at = lane - 256
        new = (lane >= 256) & (lane < 320) & (lax.rem(new_at, 32) == sample) & (
            lax.div(new_at, 32) <= step
        )
        qu = jnp.concatenate([q[0, pl.ds(128 * u, 128)], q[1, pl.ds(128 * u, 128)]], axis=0)
        s = jnp.where(cached | new, dot_t(qu, ck[u]), NEG)
        top = jnp.max(s, axis=1, keepdims=True)
        p = jnp.exp2(s * C2 - top * C2)
        own_m[u] = jnp.broadcast_to(top * SCALE, (256, HD))
        own_l[u] = jnp.broadcast_to(jnp.sum(p, axis=1, keepdims=True), (256, HD))
        own_acc[u] = dot(p.astype(BF16), cv[u])

    heads_all = tab.at[pl.ds(0, NI - 1)]
    local(heads_all, heads_all, rs.at[0]).wait()
    t4 = tab[...]
    g = HALVES * iota((NI, 4, HD), 0) + iota((NI, 4, HD), 1)
    lane3 = iota((NI, 4, HD), 2)
    first = (iota((NI, 4, HD), 1) < HALVES) & (lax.rem(g, 2) == 0)
    block = lax.div(g, 2)
    of_slot = jnp.sum(jnp.where(first & (t4 == lane3), block, 0), axis=0)
    of_block = jnp.sum(jnp.where(first & (block == lane3), t4, 0), axis=0)
    inv_v[pl.ds(0, 4)] = of_slot
    inv_v[pl.ds(4, 4)] = of_block
    to_smem = local(inv_v, inv_s, ld.at[16])
    to_smem.start()
    to_smem.wait()

    def slot_block(s):
        return jnp.clip(inv_s[0, s] + inv_s[1, s] + inv_s[2, s], 0, BLOCKS - 1)

    def block_slot(n):
        return jnp.clip(inv_s[4, n] + inv_s[5, n] + inv_s[6, n], 0, SLOTS - 1)

    local(mid, mid, rs.at[1]).wait()
    for e in range(OWN):
        def select(d, _):
            snd[e, d] = mid[slot_block(OWN * d + e)]
            return 0

        lax.fori_loop(0, NI, select, 0)
        local(snd.at[e, inst], qin.at[e, inst], rs.at[2 + e]).start()

        def send(n, _):
            d = lax.rem(inst + n, NI)
            remote(snd.at[e, d], qin.at[e, inst], ss.at[2 + e], rs.at[2 + e], inst=d).start()
            return 0

        lax.fori_loop(1, NI, send, 0)

    load_k.wait()
    load_v.wait()
    eye = iota((HD, HD), 0) == iota((HD, HD), 1)
    run_of = lax.div(iota((1, HD), 1), 16)
    for e in range(OWN):
        local(qin.at[e], qin.at[e], rs.at[2 + e]).wait()
        for y in range(2):
            qv = qin[e, pl.ds(16 * y, 16)].reshape(256, HD)
            top = None
            for c in range(KEYS // KC):
                s = dot_t(qv, kk[e, pl.ds(KC * c, KC)])
                scores[:, pl.ds(KC * c, KC)] = s
                for j in range(KC // HD):
                    part = s[:, HD * j : HD * (j + 1)]
                    top = part if top is None else jnp.maximum(top, part)
            top = jnp.max(top, axis=1, keepdims=True)
            shift = top * C2
            acc = jnp.zeros((256, 2 * HD), F32)
            for c in range(KEYS // KC):
                p = jnp.exp2(scores[:, pl.ds(KC * c, KC)] * C2 - shift)
                acc += dot(p.astype(BF16), va[e, pl.ds(KC * c, KC)])
            weight = acc[:, HD:]
            obuf[e, pl.ds(16 * y, 16)] = (acc[:, :HD] / weight).astype(BF16).reshape(16, 16, HD)
            total = top * SCALE + jnp.log(weight)
            for t in range(2):
                vec = jnp.sum(
                    jnp.where(eye, total[HD * t : HD * (t + 1)], 0.0), axis=0, keepdims=True
                )
                for m in range(8):
                    tbuf[e, 16 * y + 8 * t + m] = jnp.where(run_of == m, vec, 0.0)
        at = OWN * inst + e
        local(obuf.at[e, inst], mid2.at[at], rs.at[4]).start()
        local(tbuf.at[e, inst], tmid.at[at], rs.at[5]).start()

        def back(n, _):
            j = lax.rem(inst + n, NI)
            remote(obuf.at[e, j], mid2.at[at], ss.at[4], rs.at[4], inst=j).start()
            remote(tbuf.at[e, j], tmid.at[at], ss.at[5], rs.at[5], inst=j).start()
            return 0

        lax.fori_loop(1, NI, back, 0)

    local(mid2, mid2, rs.at[4]).wait()
    local(tmid, tmid, rs.at[5]).wait()

    def select2(n, _):
        at = block_slot(n)
        snd2[n] = mid2[at]
        tsnd[n] = tmid[at]
        return 0

    lax.fori_loop(0, BLOCKS, select2, 0)
    first_n = lax.div(HALVES * inst + 1, 2)

    def home(k, _):
        n = lax.rem(first_n + k, BLOCKS)
        gg = 2 * n + yy
        d = lax.div(gg, HALVES)
        u = lax.rem(gg, HALVES)

        @pl.when(d == inst)
        def _():
            local(snd2.at[n], pin.at[u, zz], rs.at[6]).start()
            local(tsnd.at[n], tin.at[u, zz], rs.at[7]).start()

        @pl.when(d != inst)
        def _():
            remote(snd2.at[n], pin.at[u, zz], ss.at[6], rs.at[6], inst=d).start()
            remote(tsnd.at[n], tin.at[u, zz], ss.at[7], rs.at[7], inst=d).start()

        return 0

    lax.fori_loop(0, BLOCKS, home, 0)
    load_w.wait()
    local(pin, pin, rs.at[6]).wait()
    local(tin, tin, rs.at[7]).wait()

    for u in range(HALVES):
        for t in range(2):
            vec = tin[u, 8 * t]
            for m in range(1, 8):
                vec = vec + tin[u, 8 * t + m]
            total = jnp.sum(
                jnp.where(eye, jnp.broadcast_to(vec, (HD, HD)), 0.0), axis=1, keepdims=True
            )
            rows = pl.ds(HD * t, HD)
            own_top = own_m[u, rows]
            top = jnp.maximum(total, own_top)
            carried = jnp.exp(total - top)
            own = jnp.exp(own_top - top)
            below = carried + own * own_l[u, rows]
            before = pin[u, pl.ds(8 * t, 8)].reshape(HD, HD).astype(F32)
            att[t, pl.ds(HD * u, HD)] = (carried * before + own * own_acc[u, rows]) / below
    for t in range(2):
        att[t, pl.ds(384, 16)] = jnp.zeros((16, HD), F32)

    for c in range(2):
        for a in range(8):
            k = 2 * a + c
            for h in range(4):
                pair = [att[t, pl.ds(24 * k + h, 8, stride=4)] for t in range(2)]
                lhs[pl.ds(128 * c + 16 * a, 16), pl.ds(HD * h, HD)] = jnp.concatenate(
                    pair, axis=0
                ).astype(BF16)

    kept = pl.ds(pl.multiple_of(core * 128, 128), 128)
    given = pl.ds(pl.multiple_of((1 - core) * 128, 128), 128)
    for c in range(NCH):
        cs[c] = dot(lhs[given], w[:, pl.ds(CH * c, CH)]).astype(BF16)
        remote(cs.at[c], cr.at[c], css.at[c], crs.at[c], tp=partner).start()
    for c in range(NCH):
        mine[c] = dot(lhs[kept], w[:, pl.ds(CH * c, CH)])
    for c in range(NCH):
        remote(cs.at[c], cr.at[c], css.at[c], crs.at[c], tp=partner).wait_recv()
        both = mine[c] + cr[c].astype(F32)
        sums[c] = both.reshape(8, 16, CH)
        xs[c] = both.astype(BF16).reshape(8, 16, CH)

        def spread_out(n, _):
            remote(
                xs.at[c, lax.rem(chip + n, 8)], xr.at[c, n - 1], xss.at[c], xrs.at[c], tp=chip_at(n)
            ).start()
            return 0

        lax.fori_loop(1, 8, spread_out, 0)
    for c in range(NCH):
        local(xr.at[c], xr.at[c], xrs.at[c]).wait()
        total = sums[c, chip]
        for n in range(7):
            total = total + xr[c, n].astype(F32)
        out[:, pl.ds(CH * c, CH)] = total

    for c in range(NCH):
        remote(cs.at[c], cr.at[c], css.at[c], crs.at[c], tp=partner).wait_send()
        local(xr.at[c], xr.at[c], xss.at[c]).wait()
    local(heads_all, heads_all, ss.at[0]).wait()
    for e in range(OWN):
        sent = snd.at[e, pl.ds(0, NI - 1)]
        local(sent, sent, ss.at[2 + e]).wait()
    sent = mid2.at[pl.ds(0, OWN * (NI - 1))]
    local(sent, sent, ss.at[4]).wait()
    sent = tmid.at[pl.ds(0, OWN * (NI - 1))]
    local(sent, sent, ss.at[5]).wait()
    kept_here = 1 + jnp.where(lax.rem(zz, 2) == yy, 1, 0)
    for n_kept in (1, 2):

        @pl.when(kept_here == n_kept)
        def _():
            sent = mid.at[pl.ds(0, BLOCKS - n_kept)]
            local(sent, sent, ss.at[1]).wait()
            local(sent, sent, ss.at[6]).wait()
            sent = tsnd.at[pl.ds(0, BLOCKS - n_kept)]
            local(sent, sent, ss.at[7]).wait()


def shards(
    queries,
    row_prompt,
    owner_slot,
    suffix_len,
    prefix_keys,
    prefix_values,
    suffix_keys,
    suffix_values,
    new_keys,
    new_values,
    out_weight,
):
    smem = pl.BlockSpec(memory_space=pltpu.SMEM)
    vmem = pl.BlockSpec(memory_space=pltpu.VMEM)
    hbm = pl.BlockSpec(memory_space=pl.ANY)
    sem = pltpu.SemaphoreType.DMA
    scratch = [
        pltpu.VMEM((2, 384, HD), BF16),
        pltpu.VMEM((OWN, KEYS, HD), BF16),
        pltpu.VMEM((OWN, KEYS, 2 * HD), BF16),
        pltpu.VMEM((HALVES, 384, HD), BF16),
        pltpu.VMEM((HALVES, 384, HD), BF16),
        pltpu.VMEM((512, D), BF16),
        pltpu.VMEM((NI, 4, HD), I32),
        pltpu.VMEM((8, HD), I32),
        pltpu.SMEM((8, HD), I32),
        pltpu.VMEM((BLOCKS, 16, HD), BF16),
        pltpu.VMEM((OWN, NI, 16, HD), BF16),
        pltpu.VMEM((OWN, NI, 16, HD), BF16),
        pltpu.VMEM((256, KEYS), F32),
        pltpu.VMEM((OWN, NI, 16, HD), BF16),
        pltpu.VMEM((OWN, NI, 1, HD), F32),
        pltpu.VMEM((SLOTS, 16, HD), BF16),
        pltpu.VMEM((SLOTS, 1, HD), F32),
        pltpu.VMEM((BLOCKS, 16, HD), BF16),
        pltpu.VMEM((BLOCKS, 1, HD), F32),
        pltpu.VMEM((HALVES, NZ, 16, HD), BF16),
        pltpu.VMEM((HALVES, NZ, 1, HD), F32),
        pltpu.VMEM((HALVES, 256, HD), F32),
        pltpu.VMEM((HALVES, 256, HD), F32),
        pltpu.VMEM((HALVES, 256, HD), F32),
        pltpu.VMEM((2, 400, HD), F32),
        pltpu.VMEM((256, 512), BF16),
        pltpu.VMEM((NCH, 128, CH), F32),
        pltpu.VMEM((NCH, 128, CH), BF16),
        pltpu.VMEM((NCH, 128, CH), BF16),
        pltpu.VMEM((NCH, 8, 16, CH), BF16),
        pltpu.VMEM((NCH, 7, 16, CH), BF16),
        pltpu.VMEM((NCH, 8, 16, CH), F32),
        sem((17,)),
        sem((8,)),
        sem((8,)),
        sem((NCH,)),
        sem((NCH,)),
        sem((NCH,)),
        sem((NCH,)),
    ]
    result = pl.pallas_call(
        kernel,
        out_shape=jax.ShapeDtypeStruct((16, D), F32),
        in_specs=[smem, smem, vmem] + [hbm] * 8,
        out_specs=vmem,
        scratch_shapes=scratch,
        compiler_params=pltpu.CompilerParams(
            collective_id=0, has_side_effects=True, vmem_limit_bytes=56 * 1024 * 1024
        ),
    )(
        row_prompt,
        owner_slot,
        suffix_len.reshape(1, 96),
        queries.reshape(2, 384, HD),
        prefix_keys.reshape(OWN, KEYS, HD),
        prefix_values.reshape(OWN, KEYS, HD),
        suffix_keys.reshape(768, HD),
        suffix_values.reshape(768, HD),
        new_keys.reshape(2, 96, HD),
        new_values.reshape(2, 96, HD),
        out_weight,
    )
    rows = result.reshape(2, 8, D)[:, :6]
    return jnp.swapaxes(rows, 0, 1).astype(BF16)


def solution(mesh):
    placed = (
        P(None, "inst", "tp", None),
        P("inst"),
        P(),
        P("inst"),
        P("inst", None, "tp", None),
        P("inst", None, "tp", None),
        P("inst", None, "tp", None),
        P("inst", None, "tp", None),
        P(None, "inst", "tp", None),
        P(None, "inst", "tp", None),
        P("tp", None),
    )
    return jax.shard_map(
        shards, mesh=mesh, in_specs=placed, out_specs=P(("inst", "tp"), None, None), check_vma=False
    )
```

time: 493 us -> 95.4 us (0.19)
  blocking collectives: 261 us -> 0 us
  waiting for transfers between devices: 156 us -> 0 us
  Pallas kernels: 0 us -> 92.7 us
  local copies, waits for them, and re-layouts: 35.5 us -> 0.67 us
  between operations: 18.9 us -> 0.01 us
  matrix products: 12.5 us -> 0 us
  other arithmetic: 7.46 us -> 0.93 us
    unnamed x2 -> x0, blocking collectives: 200 us -> none
    all_gather x2 -> x0, waiting for transfers between devices: 155 us -> none  [the longest x1 115 us: shards(): result_all = lax.all_gather(jnp.stack(outputs), 'inst', axis=0, tiled=True)]
    pallas_call x0 -> x1, Pallas kernels: none -> 92.7 us  [shards(): pl.pallas_call(kernel, out_shape=jax.ShapeDtypeStruct((16, D), F32), in_s...]
    all_gather x1 -> x0, blocking collectives: 60.5 us -> none  [shards(): total_all = lax.all_gather(jnp.stack(totals), 'inst', axis=0, tiled=True)]
    all_gather x2 -> x0, local copies, waits for them, and re-layouts: 15 us -> none  [the longest x1 11 us: shards(): result_all = lax.all_gather(jnp.stack(outputs), 'inst', axis=0, tiled=True)]
    dot_general x7 -> x0, matrix products: 12.5 us -> none  [the longest x2 5.05 us: prefix_part(): jnp.einsum('tbcrd,pcd->tbcrp', grouped, key_block, preferred_element_type...]
    gather x3 -> x0, local copies, waits for them, and re-layouts: 9.21 us -> none  [the longest x1 4.62 us: shards(): prefix_out = jnp.moveaxis(result_all[row_slot, :, offsets], 0, 1)]
  transfers between devices with their start and end apart: 2 -> 0, of which waited for: 2 -> 0; matrix products, arithmetic and copies ran while one was open for 4% -> 0% of each run, Pallas kernels for 0% -> 0%
where the time goes in v1:
time: 95.4 us; the launch traced here: 94.3 us
  Pallas kernels  92.7 us (97%)
    pallas_call x1, Pallas kernels, shards(): pl.pallas_call(kernel, out_shape=jax.ShapeDtypeStruct((16, D), F32), in_s...  92.7 us

profile of v1, /device:TPU:1, one launch (start us, length us, event | category | flops | bytes accessed | tf_op | source)
XLA Modules:
  0.0 94.3 jit_solution(4791003306004176998)
XLA Ops:
  0.0 92.7 %shard_map.109 = f32[16,2560]{1,0:T(8,128)} custom-call(s32[96]{0:T(128)} %row_prompt.1, s32[48]{0:T(128)} %owner_slot.1, s32[1,96]{1,0:T(1,128)} %bitcast.22, bf16[2,384,128]{2,1,0:T(8,128)(2,1)} %bitcast.17, bf16[2,4096,128]{2,1,0:T(8,128)(2,1)} %bitcast.14, bf16[2,4096,128]{2,1,0:T(8,128)(2,1)} %bitcast.15, bf16[768,128]{1,0:T(8,128)(2,1)} %bitcast.18, ...), custom_call_target="tpu_custom_call" | custom-call | tf_op jit(solution)/shard_map/pallas_call | solution.py:496
  92.7 0.9 convert_bitcast_fusion
  93.6 0.7 copy.15

commit v2 on v1

v2 whole, which is shorter than its diff:
```python
import math

import jax
import jax.numpy as jnp
from jax import lax
from jax.experimental import pallas as pl
from jax.experimental.pallas import tpu as pltpu
from jax.sharding import PartitionSpec as P

F32 = jnp.float32
BF16 = jnp.bfloat16
I32 = jnp.int32

NI = 32
NZ = 16
HALVES = 3
BLOCKS = 48
SLOTS = 64
OWN = 2
HD = 128
KEYS = 4096
D = 2560
CH = 1280
NCH = D // CH
KC = 512
U_OF = (0, 2, 1)
SCALE = 1.0 / math.sqrt(HD)
C2 = SCALE * math.log2(math.e)
NEG = -1e30


def dot_t(a, b):
    return lax.dot_general(a, b, (((1,), (1,)), ((), ())), preferred_element_type=F32)


def dot(a, b):
    return lax.dot_general(a, b, (((1,), (0,)), ((), ())), preferred_element_type=F32)


def iota(shape, dim):
    return lax.broadcasted_iota(I32, shape, dim)


def far_first(k, n):
    up = lax.rem(k + 1, 2)
    return lax.rem(n // 2 + up * lax.div(k, 2) + (1 - up) * (n - lax.div(k + 1, 2)), n)


def kernel(
    row_prompt,
    owner_slot,
    lens,
    q_hbm,
    k_hbm,
    v_hbm,
    sk_hbm,
    sv_hbm,
    nk_hbm,
    nv_hbm,
    w_hbm,
    out,
    q,
    kk,
    va,
    ck,
    cv,
    w,
    tab,
    inv_v,
    inv_s,
    mid,
    snd,
    qin,
    scores,
    obuf,
    mid2,
    snd2,
    pin,
    tall,
    own_acc,
    own_m,
    own_l,
    att,
    lhs,
    mine,
    cs,
    cr,
    xs,
    xr,
    sums,
    ld,
    ss,
    rs,
    css,
    crs,
    xss,
    xrs,
):
    inst = lax.axis_index("inst")
    tp = lax.axis_index("tp")
    yy = lax.div(inst, NZ)
    zz = lax.rem(inst, NZ)
    core = lax.rem(tp, 2)
    chip = lax.div(tp, 2)
    partner = tp + 1 - 2 * core
    my_t = lax.rem(zz, 2)
    my_m = lax.div(zz, 2)

    def remote(src, dst, s, r, **where):
        return pltpu.make_async_remote_copy(
            src_ref=src, dst_ref=dst, send_sem=s, recv_sem=r,
            device_id=where, device_id_type=pl.DeviceIdType.MESH,
        )

    def local(src, dst, s):
        return pltpu.make_async_copy(src, dst, s)

    def chip_at(step):
        return lax.rem(chip + step, 8) * 2 + core

    left = []

    def left_of(ref, sem):
        left.append(lambda: local(ref, ref, sem).wait())

    loads_q = [
        local(q_hbm.at[:, pl.ds(128 * U_OF[o], 128)], q.at[:, o], ld.at[0]) for o in range(HALVES)
    ]
    for c in loads_q:
        c.start()
    loads_own = []
    for o in range(HALVES):
        u = U_OF[o]
        for src, dst, sem in ((sk_hbm, ck, 3), (sv_hbm, cv, 4)):
            loads_own.append(
                local(src.at[pl.ds(256 * u, 256)], dst.at[o, pl.ds(0, 256)], ld.at[sem + 4 * o])
            )
        for src, dst, sem in ((nk_hbm, ck, 5), (nv_hbm, cv, 6)):
            loads_own.append(
                local(
                    src.at[:, pl.ds(32 * u, 32)],
                    dst.at[o, pl.ds(256, 64)].reshape(2, 32, HD),
                    ld.at[sem + 4 * o],
                )
            )
    for c in loads_own:
        c.start()
    load_k = local(k_hbm, kk, ld.at[1])
    load_k.start()
    load_v = local(v_hbm, va.at[:, :, pl.ds(0, HD)], ld.at[2])
    load_v.start()
    load_w = local(w_hbm, w, ld.at[15])
    load_w.start()

    barrier = pltpu.get_barrier_semaphore()

    def greet(k, _):
        z = lax.rem(zz + far_first(k, NZ), NZ)
        for y in (1 - yy, yy):
            pl.semaphore_signal(
                barrier, inc=1, device_id={"inst": y * NZ + z},
                device_id_type=pl.DeviceIdType.MESH,
            )
        return 0

    lax.fori_loop(0, NZ - 1, greet, 0)
    pl.semaphore_signal(
        barrier, inc=1, device_id={"inst": (1 - yy) * NZ + zz}, device_id_type=pl.DeviceIdType.MESH
    )

    def greet_chip(n, _):
        pl.semaphore_signal(
            barrier, inc=1, device_id={"tp": chip_at(n)}, device_id_type=pl.DeviceIdType.MESH
        )
        return 0

    lax.fori_loop(1, 8, greet_chip, 0)
    pl.semaphore_signal(
        barrier, inc=1, device_id={"tp": partner}, device_id_type=pl.DeviceIdType.MESH
    )

    lane1 = iota((1, HD), 1)
    head = jnp.zeros((1, HD), I32)
    for u in range(HALVES):
        block = lax.div(HALVES * inst + u, 2)
        first = lax.rem(HALVES * inst + u, 2) == 0
        slot = owner_slot[row_prompt[32 * u]]
        head += jnp.where((lane1 == slot) & first, block, 0)
        head += jnp.where((lane1 == SLOTS + block) & first, slot, 0)
    tab[inst] = head
    ones = jnp.ones((256, HD), BF16)

    def set_ones(n, _):
        va[lax.div(n, 16), pl.ds(pl.multiple_of(lax.rem(n, 16) * 256, 256), 256), pl.ds(HD, HD)] = ones
        return 0

    lax.fori_loop(0, 32, set_ones, 0)
    for o in range(HALVES):
        ck[o, pl.ds(320, 64)] = jnp.zeros((64, HD), BF16)
        cv[o, pl.ds(320, 64)] = jnp.zeros((64, HD), BF16)
    for c in loads_q:
        c.wait()

    pl.semaphore_wait(barrier, NI - 1 + 1 + 7)

    b_outer = lax.div(HALVES * inst, 2)
    b_inner = lax.div(HALVES * inst + 1, 2)
    side_outer = lax.rem(zz, 2)
    side_inner = 1 - side_outer

    def outer_piece(z):
        at = pl.ds(pl.multiple_of(16 * lax.div(z, 2), 16), 16)
        return q.at[lax.rem(z, 2), pl.ds(0, 2), at], mid.at[pl.ds(b_outer, 2)]

    def inner_piece(z):
        at = pl.ds(pl.multiple_of(16 * lax.div(z, 2), 16), 16)
        return q.at[lax.rem(z, 2), 2, at], mid.at[b_inner]

    def send_head(d):
        remote(tab.at[inst], tab.at[inst], ss.at[0], rs.at[0], inst=d).start()

    def send_piece(k, _):
        z = lax.rem(zz + far_first(k, NZ), NZ)
        send_head(side_outer * NZ + z)
        send_head(side_inner * NZ + z)
        remote(*outer_piece(z), ss.at[1], rs.at[1], inst=side_outer * NZ + z).start()
        remote(*inner_piece(z), ss.at[1], rs.at[1], inst=side_inner * NZ + z).start()
        return 0

    lax.fori_loop(0, NZ - 1, send_piece, 0)
    across = (1 - yy) * NZ + zz
    send_head(across)

    @pl.when(side_outer == yy)
    def _():
        local(*outer_piece(zz), rs.at[1]).start()
        remote(*inner_piece(zz), ss.at[1], rs.at[1], inst=across).start()

    @pl.when(side_outer != yy)
    def _():
        local(*inner_piece(zz), rs.at[1]).start()
        remote(*outer_piece(zz), ss.at[1], rs.at[1], inst=across).start()

    heads_all = tab.at[pl.ds(0, NI - 1)]
    left_of(heads_all, ss.at[0])
    kept_here = 1 + jnp.where(side_outer == yy, 1, 0)

    def left_halves(ref, sem):
        def wait():
            for n_kept in (1, 2):

                @pl.when(kept_here == n_kept)
                def _():
                    sent = ref.at[pl.ds(0, BLOCKS - n_kept)]
                    local(sent, sent, sem).wait()

        left.append(wait)

    left_halves(mid, ss.at[1])

    for c in loads_own:
        c.wait()
    lens_b = jnp.broadcast_to(lens[...].astype(F32), (8, 96)).astype(BF16)
    for o in range(HALVES):
        u = U_OF[o]
        at96 = iota((96, 384), 0)
        lane96 = iota((96, 384), 1)
        spread = jnp.where(at96 == 32 * u + lax.div(lane96, 8), 1.0, 0.0).astype(BF16)
        len_row = dot(lens_b, spread)[0:1]
        row = iota((256, 384), 0)
        lane = iota((256, 384), 1)
        sample = lax.div(lax.rem(row, 128), 4)
        step = lax.div(row, 128)
        cached = (lane < 256) & (lax.div(lane, 8) == sample) & (
            lax.rem(lane, 8).astype(F32) < jnp.broadcast_to(len_row, (256, 384))
        )
        new_at = lane - 256
        new = (lane >= 256) & (lane < 320) & (lax.rem(new_at, 32) == sample) & (
            lax.div(new_at, 32) <= step
        )
        qu = jnp.concatenate([q[0, o], q[1, o]], axis=0)
        s = jnp.where(cached | new, dot_t(qu, ck[o]), NEG)
        top = jnp.max(s, axis=1, keepdims=True)
        p = jnp.exp2(s * C2 - top * C2)
        own_m[o] = jnp.broadcast_to(top * SCALE, (256, HD))
        own_l[o] = jnp.broadcast_to(jnp.sum(p, axis=1, keepdims=True), (256, HD))
        own_acc[o] = dot(p.astype(BF16), cv[o])

    local(heads_all, heads_all, rs.at[0]).wait()
    inv_v[...] = jnp.sum(tab[...], axis=0)
    to_smem = local(inv_v, inv_s, ld.at[16])
    to_smem.start()
    to_smem.wait()

    def slot_block(s):
        return jnp.clip(inv_s[0, s], 0, BLOCKS - 1)

    def block_slot(n):
        return jnp.clip(inv_s[0, SLOTS + n], 0, SLOTS - 1)

    local(mid, mid, rs.at[1]).wait()

    def select(d):
        for e in range(OWN):
            snd[d, e] = mid[slot_block(OWN * d + e)]

    def to_owner(d):
        return remote(snd.at[d], qin.at[my_t, yy, my_m], ss.at[2], rs.at[2 + my_t], inst=d)

    def send_selected(k, _):
        z = lax.rem(zz + far_first(k, NZ), NZ)
        for y in (1 - yy, yy):
            d = y * NZ + z
            select(d)
            to_owner(d).start()
        return 0

    lax.fori_loop(0, NZ - 1, send_selected, 0)
    select(across)
    to_owner(across).start()
    select(inst)
    local(snd.at[inst], qin.at[my_t, yy, my_m], rs.at[2 + my_t]).start()
    left_of(snd.at[pl.ds(0, NI - 1)], ss.at[2])

    load_k.wait()
    load_v.wait()
    eye = iota((HD, HD), 0) == iota((HD, HD), 1)
    for t in range(2):
        local(qin.at[t], qin.at[t], rs.at[2 + t]).wait()
        for e in range(OWN):
            qv = qin[t, :, :, e].reshape(256, HD)
            top = None
            for c in range(KEYS // KC):
                s = dot_t(qv, kk[e, pl.ds(KC * c, KC)])
                scores[:, pl.ds(KC * c, KC)] = s
                for j in range(KC // HD):
                    part = s[:, HD * j : HD * (j + 1)]
                    top = part if top is None else jnp.maximum(top, part)
            top = jnp.max(top, axis=1, keepdims=True)
            shift = top * C2
            acc = jnp.zeros((256, 2 * HD), F32)
            for c in range(KEYS // KC):
                p = jnp.exp2(scores[:, pl.ds(KC * c, KC)] * C2 - shift)
                acc += dot(p.astype(BF16), va[e, pl.ds(KC * c, KC)])
            weight = acc[:, HD:]
            obuf[t, :, :, e] = (acc[:, :HD] / weight).astype(BF16).reshape(2, 8, 16, HD)
            total = top * SCALE + jnp.log(weight)
            for y in range(2):
                tall[8 * inst + 4 * e + 2 * t + y] = jnp.sum(
                    jnp.where(eye, total[HD * y : HD * (y + 1)], 0.0), axis=0, keepdims=True
                )
        base = lax.rem(zz + lax.rem(zz + t, 2), NZ)
        slots = mid2.at[pl.ds(OWN * inst, OWN)]

        def back(k, _):
            z = lax.rem(base + 2 * far_first(k, 8), NZ)
            for y in (1 - yy, yy):
                remote(
                    obuf.at[t, y, lax.div(z, 2)], slots, ss.at[4], rs.at[4], inst=y * NZ + z
                ).start()
            return 0

        lax.fori_loop(0, 7, back, 0)
        near = lax.div(base, 2)
        remote(
            obuf.at[t, 1 - yy, near], slots, ss.at[4], rs.at[4], inst=(1 - yy) * NZ + base
        ).start()

        @pl.when(my_t == t)
        def _():
            local(obuf.at[t, yy, near], slots, rs.at[4]).start()

        @pl.when(my_t != t)
        def _():
            remote(obuf.at[t, yy, near], slots, ss.at[4], rs.at[4], inst=yy * NZ + base).start()

    left_of(mid2.at[pl.ds(0, OWN * (NI - 1))], ss.at[4])

    def send_totals(d):
        mine8 = tall.at[pl.ds(8 * inst, 8)]
        remote(mine8, mine8, ss.at[5], rs.at[5], inst=d).start()

    def spread_totals(k, _):
        z = lax.rem(zz + far_first(k, NZ), NZ)
        for y in (1 - yy, yy):
            send_totals(y * NZ + z)
        return 0

    lax.fori_loop(0, NZ - 1, spread_totals, 0)
    send_totals(across)
    totals_all = tall.at[pl.ds(0, 8 * (NI - 1))]
    left_of(totals_all, ss.at[5])

    local(mid2, mid2, rs.at[4]).wait()

    def select2(n, _):
        snd2[n] = mid2[block_slot(n)]
        return 0

    lax.fori_loop(0, BLOCKS, select2, 0)

    def home(d, kept):
        outer = snd2.at[pl.ds(lax.div(HALVES * d, 2), 2)], pin.at[my_t, my_m, pl.ds(0, 2)]
        inner = snd2.at[lax.div(HALVES * d + 1, 2)], pin.at[my_t, my_m, 2]
        for refs, parity in ((outer, 0), (inner, 1)):

            @pl.when(lax.rem(d + yy, 2) == parity)
            def _():
                if kept:
                    local(*refs, rs.at[6 + my_t]).start()
                else:
                    remote(*refs, ss.at[6], rs.at[6 + my_t], inst=d).start()

    def send_home(k, _):
        z = lax.rem(zz + far_first(k, NZ), NZ)
        for y in (1 - yy, yy):
            home(y * NZ + z, False)
        return 0

    lax.fori_loop(0, NZ - 1, send_home, 0)
    home(across, False)
    home(inst, True)
    left_halves(snd2, ss.at[6])

    load_w.wait()
    local(totals_all, totals_all, rs.at[5]).wait()
    kept = pl.ds(pl.multiple_of(core * 64, 64), 64)
    given = pl.ds(pl.multiple_of((1 - core) * 64, 64), 64)
    for t in range(2):
        local(pin.at[t], pin.at[t], rs.at[6 + t]).wait()
        for o in range(HALVES):
            slot = block_slot(lax.div(HALVES * inst + U_OF[o], 2))
            side = side_inner if o == 2 else side_outer
            vec = tall[slot * 4 + 2 * t + side]
            total = jnp.sum(
                jnp.where(eye, jnp.broadcast_to(vec, (HD, HD)), 0.0), axis=1, keepdims=True
            )
            rows = pl.ds(HD * t, HD)
            own_top = own_m[o, rows]
            top = jnp.maximum(total, own_top)
            carried = jnp.exp(total - top)
            own = jnp.exp(own_top - top)
            below = carried + own * own_l[o, rows]
            before = pin[t, :, o].reshape(HD, HD).astype(F32)
            att[t, pl.ds(HD * U_OF[o], HD)] = (carried * before + own * own_acc[o, rows]) / below
        att[t, pl.ds(384, 16)] = jnp.zeros((16, HD), F32)
        for c in range(2):
            for a in range(0, 8, 2):
                for h in range(4):
                    pair = [att[t, pl.ds(24 * (2 * b + c) + h, 8, stride=4)] for b in (a, a + 1)]
                    lhs[t, pl.ds(64 * c + 8 * a, 16), pl.ds(HD * h, HD)] = jnp.concatenate(
                        pair, axis=0
                    ).astype(BF16)
        for c in range(NCH):
            cs[t, c] = dot(lhs[t, given], w[:, pl.ds(CH * c, CH)]).astype(BF16)
            remote(
                cs.at[t, c], cr.at[t, c], css.at[2 * t + c], crs.at[2 * t + c], tp=partner
            ).start()
        for c in range(NCH):
            mine[c] = dot(lhs[t, kept], w[:, pl.ds(CH * c, CH)])
        for c in range(NCH):
            pair_copy = remote(
                cs.at[t, c], cr.at[t, c], css.at[2 * t + c], crs.at[2 * t + c], tp=partner
            )
            pair_copy.wait_recv()
            left.append(pair_copy.wait_send)
            both = (mine[c] + cr[t, c].astype(F32)).reshape(8, 8, CH)
            both = jnp.concatenate([both[:, :, : CH // 2], both[:, :, CH // 2 :]], axis=1)
            sums[t, c] = both
            xs[t, c] = both.astype(BF16)

            def spread_out(n, _):
                remote(
                    xs.at[t, c, lax.rem(chip + n, 8)],
                    xr.at[t, c, n - 1],
                    xss.at[2 * t + c],
                    xrs.at[2 * t + c],
                    tp=chip_at(n),
                ).start()
                return 0

            lax.fori_loop(1, 8, spread_out, 0)
            left_of(xr.at[t, c], xss.at[2 * t + c])
    for t in range(2):
        for c in range(NCH):
            local(xr.at[t, c], xr.at[t, c], xrs.at[2 * t + c]).wait()
            total = sums[t, c, chip]
            for n in range(7):
                total = total + xr[t, c, n].astype(F32)
            out[t, :, pl.ds(CH * c, CH // 2)] = total[:8]
            out[t, :, pl.ds(CH * c + CH // 2, CH // 2)] = total[8:]

    for wait in left:
        wait()


def shards(
    queries,
    row_prompt,
    owner_slot,
    suffix_len,
    prefix_keys,
    prefix_values,
    suffix_keys,
    suffix_values,
    new_keys,
    new_values,
    out_weight,
):
    smem = pl.BlockSpec(memory_space=pltpu.SMEM)
    vmem = pl.BlockSpec(memory_space=pltpu.VMEM)
    hbm = pl.BlockSpec(memory_space=pl.ANY)
    sem = pltpu.SemaphoreType.DMA
    scratch = [
        pltpu.VMEM((2, HALVES, 128, HD), BF16),
        pltpu.VMEM((OWN, KEYS, HD), BF16),
        pltpu.VMEM((OWN, KEYS, 2 * HD), BF16),
        pltpu.VMEM((HALVES, 384, HD), BF16),
        pltpu.VMEM((HALVES, 384, HD), BF16),
        pltpu.VMEM((512, D), BF16),
        pltpu.VMEM((NI, 1, HD), I32),
        pltpu.VMEM((1, HD), I32),
        pltpu.SMEM((1, HD), I32),
        pltpu.VMEM((BLOCKS, 16, HD), BF16),
        pltpu.VMEM((NI, OWN, 16, HD), BF16),
        pltpu.VMEM((2, 2, 8, OWN, 16, HD), BF16),
        pltpu.VMEM((256, KEYS), F32),
        pltpu.VMEM((2, 2, 8, OWN, 16, HD), BF16),
        pltpu.VMEM((SLOTS, 16, HD), BF16),
        pltpu.VMEM((BLOCKS, 16, HD), BF16),
        pltpu.VMEM((2, 8, HALVES, 16, HD), BF16),
        pltpu.VMEM((NI * 8, 1, HD), F32),
        pltpu.VMEM((HALVES, 256, HD), F32),
        pltpu.VMEM((HALVES, 256, HD), F32),
        pltpu.VMEM((HALVES, 256, HD), F32),
        pltpu.VMEM((2, 400, HD), F32),
        pltpu.VMEM((2, 128, 512), BF16),
        pltpu.VMEM((NCH, 64, CH), F32),
        pltpu.VMEM((2, NCH, 64, CH), BF16),
        pltpu.VMEM((2, NCH, 64, CH), BF16),
        pltpu.VMEM((2, NCH, 8, 16, CH // 2), BF16),
        pltpu.VMEM((2, NCH, 7, 16, CH // 2), BF16),
        pltpu.VMEM((2, NCH, 8, 16, CH // 2), F32),
        sem((17,)),
        sem((8,)),
        sem((8,)),
        sem((2 * NCH,)),
        sem((2 * NCH,)),
        sem((2 * NCH,)),
        sem((2 * NCH,)),
    ]
    result = pl.pallas_call(
        kernel,
        out_shape=jax.ShapeDtypeStruct((2, 8, D), F32),
        in_specs=[smem, smem, vmem] + [hbm] * 8,
        out_specs=vmem,
        scratch_shapes=scratch,
        compiler_params=pltpu.CompilerParams(
            collective_id=0, has_side_effects=True, vmem_limit_bytes=56 * 1024 * 1024
        ),
    )(
        row_prompt,
        owner_slot,
        suffix_len.reshape(1, 96),
        queries.reshape(2, 384, HD),
        prefix_keys.reshape(OWN, KEYS, HD),
        prefix_values.reshape(OWN, KEYS, HD),
        suffix_keys.reshape(768, HD),
        suffix_values.reshape(768, HD),
        new_keys.reshape(2, 96, HD),
        new_values.reshape(2, 96, HD),
        out_weight,
    )
    rows = result[:, :6]
    return jnp.swapaxes(rows, 0, 1).astype(BF16)


def solution(mesh):
    placed = (
        P(None, "inst", "tp", None),
        P("inst"),
        P(),
        P("inst"),
        P("inst", None, "tp", None),
        P("inst", None, "tp", None),
        P("inst", None, "tp", None),
        P("inst", None, "tp", None),
        P(None, "inst", "tp", None),
        P(None, "inst", "tp", None),
        P("tp", None),
    )
    return jax.shard_map(
        shards, mesh=mesh, in_specs=placed, out_specs=P(("inst", "tp"), None, None), check_vma=False
    )
```

time: 95.4 us -> 92 us (0.964); the launches traced: 94.3 us -> 91.8 us
  Pallas kernels: 92.7 us -> 90.2 us
    pallas_call x1, Pallas kernels: 92.7 us -> 90.2 us  [shards(): pl.pallas_call(kernel, out_shape=jax.ShapeDtypeStruct((2, 8, D), F32), in...]
    convert_element_type x0 -> x2, local copies, waits for them, and re-layouts: none -> 1.6 us  [shards(): return jnp.swapaxes(rows, 0, 1).astype(BF16)]
where the time goes in v2:
time: 92 us; the launch traced here: 91.8 us
  Pallas kernels  90.2 us (98%)
  local copies, waits for them, and re-layouts  1.6 us (2%)
    pallas_call x1, Pallas kernels, shards(): pl.pallas_call(kernel, out_shape=jax.ShapeDtypeStruct((2, 8, D), F32), in...  90.2 us

profile of v2, /device:TPU:1, one launch (start us, length us, event | category | flops | bytes accessed | tf_op | source)
XLA Modules:
  0.0 91.8 jit_solution(3870371626306069470)
XLA Ops:
  0.0 90.2 %shard_map.109 = f32[2,8,2560]{2,1,0:T(8,128)} custom-call(s32[96]{0:T(128)} %row_prompt.1, s32[48]{0:T(128)} %owner_slot.1, s32[1,96]{1,0:T(1,128)} %bitcast.17, bf16[2,384,128]{2,1,0:T(8,128)(2,1)} %bitcast.12, bf16[2,4096,128]{2,1,0:T(8,128)(2,1)} %bitcast.10, bf16[2,4096,128]{2,1,0:T(8,128)(2,1)} %bitcast.11, bf16[768,128]{1,0:T(8,128)(2,1)} %bitcast.13, ...), custom_call_target="tpu_custom_call" | custom-call | tf_op jit(solution)/shard_map/pallas_call | solution.py:552
  90.2 0.9 %fusion = bf16[6,2,2560]{2,0,1:T(8,128)(2,1)S(1)} fusion(f32[2,8,2560]{2,1,0:T(8,128)} %shard_map.109), kind=kLoop, calls=%fused_computation.1 | loop fusion | bytes 122880 | tf_op jit(solution)/shard_map/convert_element_type | solution.py:575
  91.2 0.7 copy.12

commit v3 on v2

--- a/solution.py
+++ b/solution.py
@@ -22,7 +22,7 @@
 D = 2560
 CH = 1280
 NCH = D // CH
-KC = 512
+KC = 1024
 U_OF = (0, 2, 1)
 SCALE = 1.0 / math.sqrt(HD)
 C2 = SCALE * math.log2(math.e)
@@ -71,7 +71,6 @@
     mid,
     snd,
     qin,
-    scores,
     obuf,
     mid2,
     snd2,
@@ -219,27 +218,37 @@
     def send_head(d):
         remote(tab.at[inst], tab.at[inst], ss.at[0], rs.at[0], inst=d).start()
 
-    def send_piece(k, _):
-        z = lax.rem(zz + far_first(k, NZ), NZ)
+    def send_pieces(z):
         send_head(side_outer * NZ + z)
         send_head(side_inner * NZ + z)
         remote(*outer_piece(z), ss.at[1], rs.at[1], inst=side_outer * NZ + z).start()
         remote(*inner_piece(z), ss.at[1], rs.at[1], inst=side_inner * NZ + z).start()
-        return 0
-
-    lax.fori_loop(0, NZ - 1, send_piece, 0)
+
+    bases = [lax.rem(zz + lax.rem(zz + t, 2), NZ) for t in range(2)]
     across = (1 - yy) * NZ + zz
-    send_head(across)
-
-    @pl.when(side_outer == yy)
-    def _():
-        local(*outer_piece(zz), rs.at[1]).start()
-        remote(*inner_piece(zz), ss.at[1], rs.at[1], inst=across).start()
-
-    @pl.when(side_outer != yy)
-    def _():
-        local(*inner_piece(zz), rs.at[1]).start()
-        remote(*outer_piece(zz), ss.at[1], rs.at[1], inst=across).start()
+    for t in range(2):
+
+        def send_step(k, _):
+            send_pieces(lax.rem(bases[t] + 2 * far_first(k, 8), NZ))
+            return 0
+
+        lax.fori_loop(0, 7, send_step, 0)
+
+        @pl.when(my_t != t)
+        def _():
+            send_pieces(bases[t])
+
+        @pl.when((my_t == t) & (side_outer == yy))
+        def _():
+            send_head(across)
+            local(*outer_piece(zz), rs.at[1]).start()
+            remote(*inner_piece(zz), ss.at[1], rs.at[1], inst=across).start()
+
+        @pl.when((my_t == t) & (side_outer != yy))
+        def _():
+            send_head(across)
+            local(*inner_piece(zz), rs.at[1]).start()
+            remote(*outer_piece(zz), ss.at[1], rs.at[1], inst=across).start()
 
     heads_all = tab.at[pl.ds(0, NI - 1)]
     left_of(heads_all, ss.at[0])
@@ -329,19 +338,18 @@
         local(qin.at[t], qin.at[t], rs.at[2 + t]).wait()
         for e in range(OWN):
             qv = qin[t, :, :, e].reshape(256, HD)
-            top = None
+            top = jnp.full((256, 1), NEG, F32)
+            acc = jnp.zeros((256, 2 * HD), F32)
             for c in range(KEYS // KC):
                 s = dot_t(qv, kk[e, pl.ds(KC * c, KC)])
-                scores[:, pl.ds(KC * c, KC)] = s
-                for j in range(KC // HD):
-                    part = s[:, HD * j : HD * (j + 1)]
-                    top = part if top is None else jnp.maximum(top, part)
-            top = jnp.max(top, axis=1, keepdims=True)
-            shift = top * C2
-            acc = jnp.zeros((256, 2 * HD), F32)
-            for c in range(KEYS // KC):
-                p = jnp.exp2(scores[:, pl.ds(KC * c, KC)] * C2 - shift)
-                acc += dot(p.astype(BF16), va[e, pl.ds(KC * c, KC)])
+                part = s[:, :HD]
+                for j in range(1, KC // HD):
+                    part = jnp.maximum(part, s[:, HD * j : HD * (j + 1)])
+                higher = jnp.maximum(top, jnp.max(part, axis=1, keepdims=True))
+                p = jnp.exp2(s * C2 - higher * C2)
+                again = jnp.exp2((top - higher) * C2)
+                acc = acc * again + dot(p.astype(BF16), va[e, pl.ds(KC * c, KC)])
+                top = higher
             weight = acc[:, HD:]
             obuf[t, :, :, e] = (acc[:, :HD] / weight).astype(BF16).reshape(2, 8, 16, HD)
             total = top * SCALE + jnp.log(weight)
@@ -349,7 +357,7 @@
                 tall[8 * inst + 4 * e + 2 * t + y] = jnp.sum(
                     jnp.where(eye, total[HD * y : HD * (y + 1)], 0.0), axis=0, keepdims=True
                 )
-        base = lax.rem(zz + lax.rem(zz + t, 2), NZ)
+        base = bases[t]
         slots = mid2.at[pl.ds(OWN * inst, OWN)]
 
         def back(k, _):
@@ -424,8 +432,6 @@
 
     load_w.wait()
     local(totals_all, totals_all, rs.at[5]).wait()
-    kept = pl.ds(pl.multiple_of(core * 64, 64), 64)
-    given = pl.ds(pl.multiple_of((1 - core) * 64, 64), 64)
     for t in range(2):
         local(pin.at[t], pin.at[t], rs.at[6 + t]).wait()
         for o in range(HALVES):
@@ -452,19 +458,19 @@
                         pair, axis=0
                     ).astype(BF16)
         for c in range(NCH):
-            cs[t, c] = dot(lhs[t, given], w[:, pl.ds(CH * c, CH)]).astype(BF16)
+            part = dot(lhs[t], w[:, pl.ds(CH * c, CH)])
+            cs[t, c] = jnp.where(core == 0, part[64:], part[:64]).astype(BF16)
+            mine[t, c] = jnp.where(core == 0, part[:64], part[64:])
             remote(
                 cs.at[t, c], cr.at[t, c], css.at[2 * t + c], crs.at[2 * t + c], tp=partner
             ).start()
-        for c in range(NCH):
-            mine[c] = dot(lhs[t, kept], w[:, pl.ds(CH * c, CH)])
         for c in range(NCH):
             pair_copy = remote(
                 cs.at[t, c], cr.at[t, c], css.at[2 * t + c], crs.at[2 * t + c], tp=partner
             )
             pair_copy.wait_recv()
             left.append(pair_copy.wait_send)
-            both = (mine[c] + cr[t, c].astype(F32)).reshape(8, 8, CH)
+            both = (mine[t, c] + cr[t, c].astype(F32)).reshape(8, 8, CH)
             both = jnp.concatenate([both[:, :, : CH // 2], both[:, :, CH // 2 :]], axis=1)
             sums[t, c] = both
             xs[t, c] = both.astype(BF16)
@@ -481,14 +487,20 @@
 
             lax.fori_loop(1, 8, spread_out, 0)
             left_of(xr.at[t, c], xss.at[2 * t + c])
-    for t in range(2):
-        for c in range(NCH):
+    for c in range(NCH):
+        totals = []
+        for t in range(2):
             local(xr.at[t, c], xr.at[t, c], xrs.at[2 * t + c]).wait()
             total = sums[t, c, chip]
             for n in range(7):
                 total = total + xr[t, c, n].astype(F32)
-            out[t, :, pl.ds(CH * c, CH // 2)] = total[:8]
-            out[t, :, pl.ds(CH * c + CH // 2, CH // 2)] = total[8:]
+            totals.append(total)
+        for half in range(2):
+            for r in range(6):
+                at = 8 * half + r
+                out[r, :, pl.ds(CH * c + CH // 2 * half, CH // 2)] = jnp.concatenate(
+                    [total[at : at + 1] for total in totals], axis=0
+                ).astype(BF16)
 
     for wait in left:
         wait()
@@ -524,7 +536,6 @@
         pltpu.VMEM((BLOCKS, 16, HD), BF16),
         pltpu.VMEM((NI, OWN, 16, HD), BF16),
         pltpu.VMEM((2, 2, 8, OWN, 16, HD), BF16),
-        pltpu.VMEM((256, KEYS), F32),
         pltpu.VMEM((2, 2, 8, OWN, 16, HD), BF16),
         pltpu.VMEM((SLOTS, 16, HD), BF16),
         pltpu.VMEM((BLOCKS, 16, HD), BF16),
@@ -535,7 +546,7 @@
         pltpu.VMEM((HALVES, 256, HD), F32),
         pltpu.VMEM((2, 400, HD), F32),
         pltpu.VMEM((2, 128, 512), BF16),
-        pltpu.VMEM((NCH, 64, CH), F32),
+        pltpu.VMEM((2, NCH, 64, CH), F32),
         pltpu.VMEM((2, NCH, 64, CH), BF16),
         pltpu.VMEM((2, NCH, 64, CH), BF16),
         pltpu.VMEM((2, NCH, 8, 16, CH // 2), BF16),
@@ -549,9 +560,9 @@
         sem((2 * NCH,)),
         sem((2 * NCH,)),
     ]
-    result = pl.pallas_call(
+    return pl.pallas_call(
         kernel,
-        out_shape=jax.ShapeDtypeStruct((2, 8, D), F32),
+        out_shape=jax.ShapeDtypeStruct((6, 2, D), BF16),
         in_specs=[smem, smem, vmem] + [hbm] * 8,
         out_specs=vmem,
         scratch_shapes=scratch,
@@ -571,8 +582,6 @@
         new_values.reshape(2, 96, HD),
         out_weight,
     )
-    rows = result[:, :6]
-    return jnp.swapaxes(rows, 0, 1).astype(BF16)
 
 
 def solution(mesh):

time: 92 us -> 86.6 us (0.941)
  Pallas kernels: 90.2 us -> 84.9 us
    pallas_call x1, Pallas kernels: 90.2 us -> 84.9 us  [shards(): pl.pallas_call(kernel, out_shape=jax.ShapeDtypeStruct((6, 2, D), BF16), i...]
    convert_element_type x2 -> x0, local copies, waits for them, and re-layouts: 1.6 us -> none  [shards(): return jnp.swapaxes(rows, 0, 1).astype(BF16)]
    unnamed x0 -> x1, local copies, waits for them, and re-layouts: none -> 1.5 us
where the time goes in v3:
time: 86.6 us; the launch traced here: 86.4 us
  Pallas kernels  84.9 us (98%)
  local copies, waits for them, and re-layouts  1.5 us (2%)
    pallas_call x1, Pallas kernels, shards(): pl.pallas_call(kernel, out_shape=jax.ShapeDtypeStruct((6, 2, D), BF16), i...  84.9 us

profile of v3, /device:TPU:1, one launch (start us, length us, event | category | flops | bytes accessed | tf_op | source)
XLA Modules:
  0.0 86.4 jit_solution(4654421698788542901)
XLA Ops:
  0.0 84.9 %shard_map.109 = bf16[6,2,2560]{2,1,0:T(2,128)(2,1)} custom-call(s32[96]{0:T(128)} %row_prompt.1, s32[48]{0:T(128)} %owner_slot.1, s32[1,96]{1,0:T(1,128)} %bitcast.15, bf16[2,384,128]{2,1,0:T(8,128)(2,1)} %bitcast.10, bf16[2,4096,128]{2,1,0:T(8,128)(2,1)} %bitcast.8, bf16[2,4096,128]{2,1,0:T(8,128)(2,1)} %bitcast.9, bf16[768,128]{1,0:T(8,128)(2,1)} %bitcast.11, ...), custom_call_target="tpu_custom_call" | custom-call | tf_op jit(solution)/shard_map/pallas_call | solution.py:563
  84.9 1.5 %copy.13 = bf16[6,2,2560]{2,1,0:T(2,128)(2,1)} copy(bf16[6,2,2560]{2,1,0:T(2,128)(2,1)} %shard_map.109) | data formatting | bytes 122880

commit v4 on v3

--- a/solution.py
+++ b/solution.py
@@ -75,7 +75,11 @@
     mid2,
     snd2,
     pin,
-    tall,
+    tvec,
+    tmid,
+    tsnd,
+    spare,
+    tin,
     own_acc,
     own_m,
     own_l,
@@ -354,52 +358,42 @@
             obuf[t, :, :, e] = (acc[:, :HD] / weight).astype(BF16).reshape(2, 8, 16, HD)
             total = top * SCALE + jnp.log(weight)
             for y in range(2):
-                tall[8 * inst + 4 * e + 2 * t + y] = jnp.sum(
+                tvec[t, y, e] = jnp.sum(
                     jnp.where(eye, total[HD * y : HD * (y + 1)], 0.0), axis=0, keepdims=True
                 )
         base = bases[t]
         slots = mid2.at[pl.ds(OWN * inst, OWN)]
+        slots_t = tmid.at[pl.ds(OWN * inst, OWN)]
+
+        def back_to(y, z):
+            d = y * NZ + z
+            remote(obuf.at[t, y, lax.div(z, 2)], slots, ss.at[4], rs.at[4], inst=d).start()
+            remote(tvec.at[t, y], slots_t, ss.at[5], rs.at[5], inst=d).start()
 
         def back(k, _):
             z = lax.rem(base + 2 * far_first(k, 8), NZ)
             for y in (1 - yy, yy):
-                remote(
-                    obuf.at[t, y, lax.div(z, 2)], slots, ss.at[4], rs.at[4], inst=y * NZ + z
-                ).start()
+                back_to(y, z)
             return 0
 
         lax.fori_loop(0, 7, back, 0)
-        near = lax.div(base, 2)
-        remote(
-            obuf.at[t, 1 - yy, near], slots, ss.at[4], rs.at[4], inst=(1 - yy) * NZ + base
-        ).start()
+        back_to(1 - yy, base)
 
         @pl.when(my_t == t)
         def _():
-            local(obuf.at[t, yy, near], slots, rs.at[4]).start()
+            local(obuf.at[t, yy, my_m], slots, rs.at[4]).start()
+            local(tvec.at[t, yy], slots_t, rs.at[5]).start()
 
         @pl.when(my_t != t)
         def _():
-            remote(obuf.at[t, yy, near], slots, ss.at[4], rs.at[4], inst=yy * NZ + base).start()
+            back_to(yy, base)
 
     left_of(mid2.at[pl.ds(0, OWN * (NI - 1))], ss.at[4])
 
-    def send_totals(d):
-        mine8 = tall.at[pl.ds(8 * inst, 8)]
-        remote(mine8, mine8, ss.at[5], rs.at[5], inst=d).start()
-
-    def spread_totals(k, _):
-        z = lax.rem(zz + far_first(k, NZ), NZ)
-        for y in (1 - yy, yy):
-            send_totals(y * NZ + z)
-        return 0
-
-    lax.fori_loop(0, NZ - 1, spread_totals, 0)
-    send_totals(across)
-    totals_all = tall.at[pl.ds(0, 8 * (NI - 1))]
-    left_of(totals_all, ss.at[5])
+    left_of(tmid.at[pl.ds(0, OWN * (NI - 1))], ss.at[5])
 
     local(mid2, mid2, rs.at[4]).wait()
+    local(tmid, tmid, rs.at[5]).wait()
 
     def select2(n, _):
         snd2[n] = mid2[block_slot(n)]
@@ -430,16 +424,33 @@
     home(inst, True)
     left_halves(snd2, ss.at[6])
 
+    def total_home(i, _):
+        n = my_m + 8 * i
+        tsnd[i] = tmid[block_slot(n)]
+        d = lax.div(2 * n + yy, HALVES)
+        to = tin.at[my_t, lax.rem(2 * lax.rem(2 * n + yy, HALVES), HALVES)]
+
+        @pl.when(d == inst)
+        def _():
+            local(tsnd.at[i], to, rs.at[8 + my_t]).start()
+            local(tsnd.at[i], spare.at[i], ss.at[7]).start()
+
+        @pl.when(d != inst)
+        def _():
+            remote(tsnd.at[i], to, ss.at[7], rs.at[8 + my_t], inst=d).start()
+
+        return 0
+
+    lax.fori_loop(0, BLOCKS // 8, total_home, 0)
+    left_of(tsnd, ss.at[7])
+
     load_w.wait()
-    local(totals_all, totals_all, rs.at[5]).wait()
     for t in range(2):
         local(pin.at[t], pin.at[t], rs.at[6 + t]).wait()
+        local(tin.at[t], tin.at[t], rs.at[8 + t]).wait()
         for o in range(HALVES):
-            slot = block_slot(lax.div(HALVES * inst + U_OF[o], 2))
-            side = side_inner if o == 2 else side_outer
-            vec = tall[slot * 4 + 2 * t + side]
             total = jnp.sum(
-                jnp.where(eye, jnp.broadcast_to(vec, (HD, HD)), 0.0), axis=1, keepdims=True
+                jnp.where(eye, jnp.broadcast_to(tin[t, o], (HD, HD)), 0.0), axis=1, keepdims=True
             )
             rows = pl.ds(HD * t, HD)
             own_top = own_m[o, rows]
@@ -540,7 +551,11 @@
         pltpu.VMEM((SLOTS, 16, HD), BF16),
         pltpu.VMEM((BLOCKS, 16, HD), BF16),
         pltpu.VMEM((2, 8, HALVES, 16, HD), BF16),
-        pltpu.VMEM((NI * 8, 1, HD), F32),
+        pltpu.VMEM((2, 2, OWN, 1, HD), F32),
+        pltpu.VMEM((SLOTS, 1, HD), F32),
+        pltpu.VMEM((BLOCKS // 8, 1, HD), F32),
+        pltpu.VMEM((BLOCKS // 8, 1, HD), F32),
+        pltpu.VMEM((2, HALVES, 1, HD), F32),
         pltpu.VMEM((HALVES, 256, HD), F32),
         pltpu.VMEM((HALVES, 256, HD), F32),
         pltpu.VMEM((HALVES, 256, HD), F32),
@@ -554,7 +569,7 @@
         pltpu.VMEM((2, NCH, 8, 16, CH // 2), F32),
         sem((17,)),
         sem((8,)),
-        sem((8,)),
+        sem((10,)),
         sem((2 * NCH,)),
         sem((2 * NCH,)),
         sem((2 * NCH,)),

time: 86.6 us -> 81.6 us (0.942)
  Pallas kernels: 84.9 us -> 80 us
    pallas_call x1, Pallas kernels: 84.9 us -> 80 us  [shards(): pl.pallas_call(kernel, out_shape=jax.ShapeDtypeStruct((6, 2, D), BF16), i...]
where the time goes in v4:
time: 81.6 us; the launch traced here: 81.5 us
  Pallas kernels  80 us (98%)
  local copies, waits for them, and re-layouts  1.5 us (2%)
    pallas_call x1, Pallas kernels, shards(): pl.pallas_call(kernel, out_shape=jax.ShapeDtypeStruct((6, 2, D), BF16), i...  80 us

profile of v4, /device:TPU:1, one launch (start us, length us, event | category | flops | bytes accessed | tf_op | source)
XLA Modules:
  0.0 81.5 jit_solution(4157577758015667514)
XLA Ops:
  0.0 80.0 %shard_map.109 = bf16[6,2,2560]{2,1,0:T(2,128)(2,1)} custom-call(s32[96]{0:T(128)} %row_prompt.1, s32[48]{0:T(128)} %owner_slot.1, s32[1,96]{1,0:T(1,128)} %bitcast.15, bf16[2,384,128]{2,1,0:T(8,128)(2,1)} %bitcast.10, bf16[2,4096,128]{2,1,0:T(8,128)(2,1)} %bitcast.8, bf16[2,4096,128]{2,1,0:T(8,128)(2,1)} %bitcast.9, bf16[768,128]{1,0:T(8,128)(2,1)} %bitcast.11, ...), custom_call_target="tpu_custom_call" | custom-call | tf_op jit(solution)/shard_map/pallas_call | solution.py:578
  80.0 1.5 %copy.13 = bf16[6,2,2560]{2,1,0:T(2,128)(2,1)} copy(bf16[6,2,2560]{2,1,0:T(2,128)(2,1)} %shard_map.109) | data formatting | bytes 122880

commit v5 on v4

--- a/solution.py
+++ b/solution.py
@@ -16,6 +16,7 @@
 HALVES = 3
 BLOCKS = 48
 SLOTS = 64
+EARLY = 4
 OWN = 2
 HD = 128
 KEYS = 4096
@@ -91,6 +92,7 @@
     xs,
     xr,
     sums,
+    step0,
     ld,
     ss,
     rs,
@@ -108,6 +110,7 @@
     partner = tp + 1 - 2 * core
     my_t = lax.rem(zz, 2)
     my_m = lax.div(zz, 2)
+    has_totals = lax.rem(zz, 8) < 2
 
     def remote(src, dst, s, r, **where):
         return pltpu.make_async_remote_copy(
@@ -368,7 +371,10 @@
         def back_to(y, z):
             d = y * NZ + z
             remote(obuf.at[t, y, lax.div(z, 2)], slots, ss.at[4], rs.at[4], inst=d).start()
-            remote(tvec.at[t, y], slots_t, ss.at[5], rs.at[5], inst=d).start()
+
+            @pl.when(lax.rem(z, 8) < 2)
+            def _():
+                remote(tvec.at[t, y], slots_t, ss.at[5], rs.at[5], inst=d).start()
 
         def back(k, _):
             z = lax.rem(base + 2 * far_first(k, 8), NZ)
@@ -382,7 +388,11 @@
         @pl.when(my_t == t)
         def _():
             local(obuf.at[t, yy, my_m], slots, rs.at[4]).start()
-            local(tvec.at[t, yy], slots_t, rs.at[5]).start()
+
+            @pl.when(has_totals)
+            def _():
+                local(tvec.at[t, yy], slots_t, rs.at[5]).start()
+                local(tvec.at[t, yy], spare.at[pl.ds(BLOCKS // 2, OWN)], ss.at[5]).start()
 
         @pl.when(my_t != t)
         def _():
@@ -390,59 +400,78 @@
 
     left_of(mid2.at[pl.ds(0, OWN * (NI - 1))], ss.at[4])
 
-    left_of(tmid.at[pl.ds(0, OWN * (NI - 1))], ss.at[5])
+    left_of(tmid.at[pl.ds(0, OWN * 8)], ss.at[5])
 
     local(mid2, mid2, rs.at[4]).wait()
-    local(tmid, tmid, rs.at[5]).wait()
-
-    def select2(n, _):
-        snd2[n] = mid2[block_slot(n)]
-        return 0
-
-    lax.fori_loop(0, BLOCKS, select2, 0)
-
-    def home(d, kept):
-        outer = snd2.at[pl.ds(lax.div(HALVES * d, 2), 2)], pin.at[my_t, my_m, pl.ds(0, 2)]
-        inner = snd2.at[lax.div(HALVES * d + 1, 2)], pin.at[my_t, my_m, 2]
-        for refs, parity in ((outer, 0), (inner, 1)):
+
+    def home(d):
+        n0, n1 = lax.div(HALVES * d, 2), lax.div(HALVES * d + 1, 2)
+        outer = (n0, n0 + 1), snd2.at[pl.ds(n0, 2)], pin.at[my_t, my_m, pl.ds(0, 2)]
+        inner = (n1,), snd2.at[n1], pin.at[my_t, my_m, 2]
+        for (blocks, src, dst), parity in ((outer, 0), (inner, 1)):
 
             @pl.when(lax.rem(d + yy, 2) == parity)
             def _():
-                if kept:
-                    local(*refs, rs.at[6 + my_t]).start()
-                else:
-                    remote(*refs, ss.at[6], rs.at[6 + my_t], inst=d).start()
-
-    def send_home(k, _):
+                for n in blocks:
+                    snd2[n] = mid2[block_slot(n)]
+
+                @pl.when(d == inst)
+                def _():
+                    local(src, dst, rs.at[6 + my_t]).start()
+
+                @pl.when(d != inst)
+                def _():
+                    remote(src, dst, ss.at[6], rs.at[6 + my_t], inst=d).start()
+
+    def home_first(z, _):
+        for y in (1 - yy, yy):
+            home(y * NZ + z)
+        return 0
+
+    lax.fori_loop(0, EARLY, home_first, 0)
+
+    def home_others(k, _):
         z = lax.rem(zz + far_first(k, NZ), NZ)
-        for y in (1 - yy, yy):
-            home(y * NZ + z, False)
+
+        @pl.when(z >= EARLY)
+        def _():
+            for y in (1 - yy, yy):
+                home(y * NZ + z)
+
         return 0
 
-    lax.fori_loop(0, NZ - 1, send_home, 0)
-    home(across, False)
-    home(inst, True)
+    @pl.when(has_totals)
+    def _():
+        local(tmid, tmid, rs.at[5]).wait()
+
+        def total_home(i, _):
+            n = lax.div(my_m, 4) + 2 * i
+            tsnd[i] = tmid[block_slot(n)]
+            d = lax.div(2 * n + yy, HALVES)
+            to = tin.at[my_t, lax.rem(2 * lax.rem(2 * n + yy, HALVES), HALVES)]
+
+            @pl.when(d == inst)
+            def _():
+                local(tsnd.at[i], to, rs.at[8 + my_t]).start()
+                local(tsnd.at[i], spare.at[i], ss.at[7]).start()
+
+            @pl.when(d != inst)
+            def _():
+                remote(tsnd.at[i], to, ss.at[7], rs.at[8 + my_t], inst=d).start()
+
+            return 0
+
+        lax.fori_loop(0, BLOCKS // 2, total_home, 0)
+
+    lax.fori_loop(0, NZ, home_others, 0)
     left_halves(snd2, ss.at[6])
 
-    def total_home(i, _):
-        n = my_m + 8 * i
-        tsnd[i] = tmid[block_slot(n)]
-        d = lax.div(2 * n + yy, HALVES)
-        to = tin.at[my_t, lax.rem(2 * lax.rem(2 * n + yy, HALVES), HALVES)]
-
-        @pl.when(d == inst)
+    def left_totals():
+        @pl.when(has_totals)
         def _():
-            local(tsnd.at[i], to, rs.at[8 + my_t]).start()
-            local(tsnd.at[i], spare.at[i], ss.at[7]).start()
-
-        @pl.when(d != inst)
-        def _():
-            remote(tsnd.at[i], to, ss.at[7], rs.at[8 + my_t], inst=d).start()
-
-        return 0
-
-    lax.fori_loop(0, BLOCKS // 8, total_home, 0)
-    left_of(tsnd, ss.at[7])
+            local(tsnd, tsnd, ss.at[7]).wait()
+
+    left.append(left_totals)
 
     load_w.wait()
     for t in range(2):
@@ -498,23 +527,23 @@
 
             lax.fori_loop(1, 8, spread_out, 0)
             left_of(xr.at[t, c], xss.at[2 * t + c])
-    for c in range(NCH):
-        totals = []
-        for t in range(2):
+    for wait in left:
+        wait()
+    for t in range(2):
+        for c in range(NCH):
             local(xr.at[t, c], xr.at[t, c], xrs.at[2 * t + c]).wait()
             total = sums[t, c, chip]
             for n in range(7):
                 total = total + xr[t, c, n].astype(F32)
-            totals.append(total)
-        for half in range(2):
-            for r in range(6):
-                at = 8 * half + r
-                out[r, :, pl.ds(CH * c + CH // 2 * half, CH // 2)] = jnp.concatenate(
-                    [total[at : at + 1] for total in totals], axis=0
-                ).astype(BF16)
-
-    for wait in left:
-        wait()
+            if t == 0:
+                step0[c] = total
+                continue
+            for half in range(2):
+                for r in range(6):
+                    at = 8 * half + r
+                    out[r, :, pl.ds(CH * c + CH // 2 * half, CH // 2)] = jnp.concatenate(
+                        [step0[c, pl.ds(at, 1)], total[at : at + 1]], axis=0
+                    ).astype(BF16)
 
 
 def shards(
@@ -553,8 +582,8 @@
         pltpu.VMEM((2, 8, HALVES, 16, HD), BF16),
         pltpu.VMEM((2, 2, OWN, 1, HD), F32),
         pltpu.VMEM((SLOTS, 1, HD), F32),
-        pltpu.VMEM((BLOCKS // 8, 1, HD), F32),
-        pltpu.VMEM((BLOCKS // 8, 1, HD), F32),
+        pltpu.VMEM((BLOCKS // 2, 1, HD), F32),
+        pltpu.VMEM((BLOCKS // 2 + OWN, 1, HD), F32),
         pltpu.VMEM((2, HALVES, 1, HD), F32),
         pltpu.VMEM((HALVES, 256, HD), F32),
         pltpu.VMEM((HALVES, 256, HD), F32),
@@ -567,6 +596,7 @@
         pltpu.VMEM((2, NCH, 8, 16, CH // 2), BF16),
         pltpu.VMEM((2, NCH, 7, 16, CH // 2), BF16),
         pltpu.VMEM((2, NCH, 8, 16, CH // 2), F32),
+        pltpu.VMEM((NCH, 16, CH // 2), F32),
         sem((17,)),
         sem((8,)),
         sem((10,)),

time: 81.6 us -> 79.7 us (0.977)
  Pallas kernels: 80 us -> 78 us
    pallas_call x1, Pallas kernels: 80 us -> 78 us  [shards(): pl.pallas_call(kernel, out_shape=jax.ShapeDtypeStruct((6, 2, D), BF16), i...]
where the time goes in v5:
time: 79.7 us; the launch traced here: 79.5 us
  Pallas kernels  78 us (98%)
  local copies, waits for them, and re-layouts  1.5 us (2%)
    pallas_call x1, Pallas kernels, shards(): pl.pallas_call(kernel, out_shape=jax.ShapeDtypeStruct((6, 2, D), BF16), i...  78 us

profile of v5, /device:TPU:1, one launch (start us, length us, event | category | flops | bytes accessed | tf_op | source)
XLA Modules:
  0.0 79.5 jit_solution(1039461948666226431)
XLA Ops:
  0.0 78.0 %shard_map.109 = bf16[6,2,2560]{2,1,0:T(2,128)(2,1)} custom-call(s32[96]{0:T(128)} %row_prompt.1, s32[48]{0:T(128)} %owner_slot.1, s32[1,96]{1,0:T(1,128)} %bitcast.15, bf16[2,384,128]{2,1,0:T(8,128)(2,1)} %bitcast.10, bf16[2,4096,128]{2,1,0:T(8,128)(2,1)} %bitcast.8, bf16[2,4096,128]{2,1,0:T(8,128)(2,1)} %bitcast.9, bf16[768,128]{1,0:T(8,128)(2,1)} %bitcast.11, ...), custom_call_target="tpu_custom_call" | custom-call | tf_op jit(solution)/shard_map/pallas_call | solution.py:608
  78.0 1.5 %copy.13 = bf16[6,2,2560]{2,1,0:T(2,128)(2,1)} copy(bf16[6,2,2560]{2,1,0:T(2,128)(2,1)} %shard_map.109) | data formatting | bytes 122880

commit v6 on v5

--- a/solution.py
+++ b/solution.py
@@ -16,6 +16,7 @@
 HALVES = 3
 BLOCKS = 48
 SLOTS = 64
+CHIPS = ((2, 1), (2, 0), (1, 1), (3, 1), (1, 0), (3, 0), (0, 1))
 EARLY = 4
 OWN = 2
 HD = 128
@@ -23,6 +24,7 @@
 D = 2560
 CH = 1280
 NCH = D // CH
+PK = 512
 KC = 1024
 U_OF = (0, 2, 1)
 SCALE = 1.0 / math.sqrt(HD)
@@ -48,9 +50,9 @@
 
 
 def kernel(
-    row_prompt,
-    owner_slot,
-    lens,
+    rp_hbm,
+    os_hbm,
+    lens_hbm,
     q_hbm,
     k_hbm,
     v_hbm,
@@ -60,6 +62,9 @@
     nv_hbm,
     w_hbm,
     out,
+    row_prompt,
+    owner_slot,
+    lens,
     q,
     kk,
     va,
@@ -129,6 +134,39 @@
     def left_of(ref, sem):
         left.append(lambda: local(ref, ref, sem).wait())
 
+    barrier = pltpu.get_barrier_semaphore()
+
+    def greet(k, _):
+        z = lax.rem(zz + far_first(k, NZ), NZ)
+        for y in (1 - yy, yy):
+            pl.semaphore_signal(
+                barrier, inc=1, device_id={"inst": y * NZ + z},
+                device_id_type=pl.DeviceIdType.MESH,
+            )
+        return 0
+
+    lax.fori_loop(0, NZ - 1, greet, 0)
+    pl.semaphore_signal(
+        barrier, inc=1, device_id={"inst": (1 - yy) * NZ + zz}, device_id_type=pl.DeviceIdType.MESH
+    )
+
+    def greet_chip(n, _):
+        pl.semaphore_signal(
+            barrier, inc=1, device_id={"tp": chip_at(n)}, device_id_type=pl.DeviceIdType.MESH
+        )
+        return 0
+
+    lax.fori_loop(1, 8, greet_chip, 0)
+    pl.semaphore_signal(
+        barrier, inc=1, device_id={"tp": partner}, device_id_type=pl.DeviceIdType.MESH
+    )
+
+    loads_t = [
+        local(rp_hbm, row_prompt, ld.at[17]),
+        local(os_hbm, owner_slot, ld.at[18]),
+    ]
+    for c in loads_t:
+        c.start()
     loads_q = [
         local(q_hbm.at[:, pl.ds(128 * U_OF[o], 128)], q.at[:, o], ld.at[0]) for o in range(HALVES)
     ]
@@ -149,6 +187,7 @@
                     ld.at[sem + 4 * o],
                 )
             )
+    loads_own.append(local(lens_hbm, lens, ld.at[19]))
     for c in loads_own:
         c.start()
     load_k = local(k_hbm, kk, ld.at[1])
@@ -158,33 +197,8 @@
     load_w = local(w_hbm, w, ld.at[15])
     load_w.start()
 
-    barrier = pltpu.get_barrier_semaphore()
-
-    def greet(k, _):
-        z = lax.rem(zz + far_first(k, NZ), NZ)
-        for y in (1 - yy, yy):
-            pl.semaphore_signal(
-                barrier, inc=1, device_id={"inst": y * NZ + z},
-                device_id_type=pl.DeviceIdType.MESH,
-            )
-        return 0
-
-    lax.fori_loop(0, NZ - 1, greet, 0)
-    pl.semaphore_signal(
-        barrier, inc=1, device_id={"inst": (1 - yy) * NZ + zz}, device_id_type=pl.DeviceIdType.MESH
-    )
-
-    def greet_chip(n, _):
-        pl.semaphore_signal(
-            barrier, inc=1, device_id={"tp": chip_at(n)}, device_id_type=pl.DeviceIdType.MESH
-        )
-        return 0
-
-    lax.fori_loop(1, 8, greet_chip, 0)
-    pl.semaphore_signal(
-        barrier, inc=1, device_id={"tp": partner}, device_id_type=pl.DeviceIdType.MESH
-    )
-
+    for c in loads_t:
+        c.wait()
     lane1 = iota((1, HD), 1)
     head = jnp.zeros((1, HD), I32)
     for u in range(HALVES):
@@ -511,21 +525,21 @@
             pair_copy.wait_recv()
             left.append(pair_copy.wait_send)
             both = (mine[t, c] + cr[t, c].astype(F32)).reshape(8, 8, CH)
-            both = jnp.concatenate([both[:, :, : CH // 2], both[:, :, CH // 2 :]], axis=1)
+            rest = both[:, :, 2 * PK :]
+            rest = jnp.concatenate([rest[:, :4], rest[:, 4:8]], axis=2)
+            both = jnp.concatenate([both[:, :6, :PK], both[:, :6, PK : 2 * PK], rest], axis=1)
             sums[t, c] = both
             xs[t, c] = both.astype(BF16)
 
-            def spread_out(n, _):
+            for n, (dx, dy) in enumerate(CHIPS):
+                to = lax.rem(lax.div(chip, 2) + dx, 4) * 2 + lax.rem(chip + dy, 2)
                 remote(
-                    xs.at[t, c, lax.rem(chip + n, 8)],
-                    xr.at[t, c, n - 1],
+                    xs.at[t, c, to],
+                    xr.at[t, c, n],
                     xss.at[2 * t + c],
                     xrs.at[2 * t + c],
-                    tp=chip_at(n),
+                    tp=2 * to + core,
                 ).start()
-                return 0
-
-            lax.fori_loop(1, 8, spread_out, 0)
             left_of(xr.at[t, c], xss.at[2 * t + c])
     for wait in left:
         wait()
@@ -538,11 +552,19 @@
             if t == 0:
                 step0[c] = total
                 continue
-            for half in range(2):
-                for r in range(6):
-                    at = 8 * half + r
-                    out[r, :, pl.ds(CH * c + CH // 2 * half, CH // 2)] = jnp.concatenate(
-                        [step0[c, pl.ds(at, 1)], total[at : at + 1]], axis=0
+            for r in range(6):
+                last = (12 + r, 0) if r < 4 else (8 + r, PK // 2)
+                for at, lane, to, width in (
+                    (r, 0, 0, PK),
+                    (6 + r, 0, PK, PK),
+                    (*last, 2 * PK, PK // 2),
+                ):
+                    out[r, :, pl.ds(CH * c + to, width)] = jnp.concatenate(
+                        [
+                            step0[c, pl.ds(at, 1), pl.ds(lane, width)],
+                            total[at : at + 1, lane : lane + width],
+                        ],
+                        axis=0,
                     ).astype(BF16)
 
 
@@ -559,11 +581,13 @@
     new_values,
     out_weight,
 ):
-    smem = pl.BlockSpec(memory_space=pltpu.SMEM)
     vmem = pl.BlockSpec(memory_space=pltpu.VMEM)
     hbm = pl.BlockSpec(memory_space=pl.ANY)
     sem = pltpu.SemaphoreType.DMA
     scratch = [
+        pltpu.SMEM((96,), I32),
+        pltpu.SMEM((48,), I32),
+        pltpu.VMEM((1, 96), I32),
         pltpu.VMEM((2, HALVES, 128, HD), BF16),
         pltpu.VMEM((OWN, KEYS, HD), BF16),
         pltpu.VMEM((OWN, KEYS, 2 * HD), BF16),
@@ -593,11 +617,11 @@
         pltpu.VMEM((2, NCH, 64, CH), F32),
         pltpu.VMEM((2, NCH, 64, CH), BF16),
         pltpu.VMEM((2, NCH, 64, CH), BF16),
-        pltpu.VMEM((2, NCH, 8, 16, CH // 2), BF16),
-        pltpu.VMEM((2, NCH, 7, 16, CH // 2), BF16),
-        pltpu.VMEM((2, NCH, 8, 16, CH // 2), F32),
-        pltpu.VMEM((NCH, 16, CH // 2), F32),
-        sem((17,)),
+        pltpu.VMEM((2, NCH, 8, 16, PK), BF16),
+        pltpu.VMEM((2, NCH, 7, 16, PK), BF16),
+        pltpu.VMEM((2, NCH, 8, 16, PK), F32),
+        pltpu.VMEM((NCH, 16, PK), F32),
+        sem((20,)),
         sem((8,)),
         sem((10,)),
         sem((2 * NCH,)),
@@ -608,7 +632,7 @@
     return pl.pallas_call(
         kernel,
         out_shape=jax.ShapeDtypeStruct((6, 2, D), BF16),
-        in_specs=[smem, smem, vmem] + [hbm] * 8,
+        in_specs=[hbm] * 11,
         out_specs=vmem,
         scratch_shapes=scratch,
         compiler_params=pltpu.CompilerParams(

time: 79.7 us -> 78 us (0.979)
  Pallas kernels: 78 us -> 76.4 us
    pallas_call x1, Pallas kernels: 78 us -> 76.4 us  [shards(): pl.pallas_call(kernel, out_shape=jax.ShapeDtypeStruct((6, 2, D), BF16), i...]
where the time goes in v6:
time: 78 us; the launch traced here: 77.9 us
  Pallas kernels  76.4 us (98%)
  local copies, waits for them, and re-layouts  1.5 us (2%)
    pallas_call x1, Pallas kernels, shards(): pl.pallas_call(kernel, out_shape=jax.ShapeDtypeStruct((6, 2, D), BF16), i...  76.4 us

profile of v6, /device:TPU:1, one launch (start us, length us, event | category | flops | bytes accessed | tf_op | source)
XLA Modules:
  0.0 77.9 jit_solution(15555193227441146167)
XLA Ops:
  0.0 76.4 %shard_map.109 = bf16[6,2,2560]{2,1,0:T(2,128)(2,1)} custom-call(s32[96]{0:T(128)} %rp_hbm.1, s32[48]{0:T(128)} %os_hbm.1, s32[1,96]{1,0:T(1,128)} %bitcast.15, bf16[2,384,128]{2,1,0:T(8,128)(2,1)} %bitcast.10, bf16[2,4096,128]{2,1,0:T(8,128)(2,1)} %bitcast.8, bf16[2,4096,128]{2,1,0:T(8,128)(2,1)} %bitcast.9, bf16[768,128]{1,0:T(8,128)(2,1)} %bitcast.11, ...), custom_call_target="tpu_custom_call" | custom-call | tf_op jit(solution)/shard_map/pallas_call | solution.py:632
  76.4 1.5 %copy.13 = bf16[6,2,2560]{2,1,0:T(2,128)(2,1)} copy(bf16[6,2,2560]{2,1,0:T(2,128)(2,1)} %shard_map.109) | data formatting | bytes 122880

commit v7 on v6

--- a/solution.py
+++ b/solution.py
@@ -115,7 +115,7 @@
     partner = tp + 1 - 2 * core
     my_t = lax.rem(zz, 2)
     my_m = lax.div(zz, 2)
-    has_totals = lax.rem(zz, 8) < 2
+    has_totals = lax.rem(zz, 8) < 4
 
     def remote(src, dst, s, r, **where):
         return pltpu.make_async_remote_copy(
@@ -386,7 +386,7 @@
             d = y * NZ + z
             remote(obuf.at[t, y, lax.div(z, 2)], slots, ss.at[4], rs.at[4], inst=d).start()
 
-            @pl.when(lax.rem(z, 8) < 2)
+            @pl.when(lax.rem(z, 8) < 4)
             def _():
                 remote(tvec.at[t, y], slots_t, ss.at[5], rs.at[5], inst=d).start()
 
@@ -406,7 +406,7 @@
             @pl.when(has_totals)
             def _():
                 local(tvec.at[t, yy], slots_t, rs.at[5]).start()
-                local(tvec.at[t, yy], spare.at[pl.ds(BLOCKS // 2, OWN)], ss.at[5]).start()
+                local(tvec.at[t, yy], spare.at[pl.ds(BLOCKS // 4, OWN)], ss.at[5]).start()
 
         @pl.when(my_t != t)
         def _():
@@ -414,7 +414,7 @@
 
     left_of(mid2.at[pl.ds(0, OWN * (NI - 1))], ss.at[4])
 
-    left_of(tmid.at[pl.ds(0, OWN * 8)], ss.at[5])
+    left_of(tmid.at[pl.ds(0, OWN * 16)], ss.at[5])
 
     local(mid2, mid2, rs.at[4]).wait()
 
@@ -459,7 +459,7 @@
         local(tmid, tmid, rs.at[5]).wait()
 
         def total_home(i, _):
-            n = lax.div(my_m, 4) + 2 * i
+            n = 2 * lax.div(my_m, 4) + lax.rem(my_m, 2) + 4 * i
             tsnd[i] = tmid[block_slot(n)]
             d = lax.div(2 * n + yy, HALVES)
             to = tin.at[my_t, lax.rem(2 * lax.rem(2 * n + yy, HALVES), HALVES)]
@@ -475,7 +475,7 @@
 
             return 0
 
-        lax.fori_loop(0, BLOCKS // 2, total_home, 0)
+        lax.fori_loop(0, BLOCKS // 4, total_home, 0)
 
     lax.fori_loop(0, NZ, home_others, 0)
     left_halves(snd2, ss.at[6])
@@ -606,8 +606,8 @@
         pltpu.VMEM((2, 8, HALVES, 16, HD), BF16),
         pltpu.VMEM((2, 2, OWN, 1, HD), F32),
         pltpu.VMEM((SLOTS, 1, HD), F32),
-        pltpu.VMEM((BLOCKS // 2, 1, HD), F32),
-        pltpu.VMEM((BLOCKS // 2 + OWN, 1, HD), F32),
+        pltpu.VMEM((BLOCKS // 4, 1, HD), F32),
+        pltpu.VMEM((BLOCKS // 4 + OWN, 1, HD), F32),
         pltpu.VMEM((2, HALVES, 1, HD), F32),
         pltpu.VMEM((HALVES, 256, HD), F32),
         pltpu.VMEM((HALVES, 256, HD), F32),

time: 78 us -> 78.9 us (1.012)
  Pallas kernels: 76.4 us -> 77.3 us
    pallas_call x1, Pallas kernels: 76.4 us -> 77.3 us  [shards(): pl.pallas_call(kernel, out_shape=jax.ShapeDtypeStruct((6, 2, D), BF16), i...]
where the time goes in v7:
time: 78.9 us; the launch traced here: 78.8 us
  Pallas kernels  77.3 us (98%)
  local copies, waits for them, and re-layouts  1.5 us (2%)
    pallas_call x1, Pallas kernels, shards(): pl.pallas_call(kernel, out_shape=jax.ShapeDtypeStruct((6, 2, D), BF16), i...  77.3 us

profile of v7, /device:TPU:1, one launch (start us, length us, event | category | flops | bytes accessed | tf_op | source)
XLA Modules:
  0.0 78.8 jit_solution(15330592607776111407)
XLA Ops:
  0.0 77.3 %shard_map.109 = bf16[6,2,2560]{2,1,0:T(2,128)(2,1)} custom-call(s32[96]{0:T(128)} %rp_hbm.1, s32[48]{0:T(128)} %os_hbm.1, s32[1,96]{1,0:T(1,128)} %bitcast.15, bf16[2,384,128]{2,1,0:T(8,128)(2,1)} %bitcast.10, bf16[2,4096,128]{2,1,0:T(8,128)(2,1)} %bitcast.8, bf16[2,4096,128]{2,1,0:T(8,128)(2,1)} %bitcast.9, bf16[768,128]{1,0:T(8,128)(2,1)} %bitcast.11, ...), custom_call_target="tpu_custom_call" | custom-call | tf_op jit(solution)/shard_map/pallas_call | solution.py:632
  77.3 1.5 %copy.13 = bf16[6,2,2560]{2,1,0:T(2,128)(2,1)} copy(bf16[6,2,2560]{2,1,0:T(2,128)(2,1)} %shard_map.109) | data formatting | bytes 122880
